TPU v7x, 256 devices: a whole 4x4x8 slice. The times are simulated.
256 devices in a mesh: inst: 32 (over y, z), tp: 8 (over x, core).
Axes of the slice: x: 4, y: 4, z: 8, core: 2. Of those that a mesh axis runs over, the one named last changes fastest.
Arguments:
- query: bfloat16 [256, 64, 128], P('inst', 'tp'), may hold values from -33 to 33
- new_key: bfloat16 [256, 8, 128], P('inst', 'tp'), may hold values from -6 to 6
- new_value: bfloat16 [256, 8, 128], P('inst', 'tp'), may hold values from -10 to 10
- key_cache: bfloat16 [1024, 256, 8, 128], P('inst', None, 'tp'), may hold values from -8 to 8
- value_cache: bfloat16 [1024, 256, 8, 128], P('inst', None, 'tp'), may hold values from -10 to 10
- out_weight: bfloat16 [8192, 4096], P('tp'), may hold values from -0.09375 to 0.09375
- lengths: int32 [256], replicated, may hold values from 1 to 4096, as said below
- block_owner: int32 [1024], P('inst'), may hold values from -1 to 255, as said below
- block_index: int32 [1024], P('inst'), may hold values from 0 to 15, as said below
Outputs:
- mixed: bfloat16 [256, 4096], P('inst', 'tp')
Inputs may be any that keep to these rules, and one draw needn't show every extreme that they name: `lengths`: requests of instance i are rows i * 8 to i * 8 + 7. Some request holds exactly 4096 tokens and some holds 1. `block_owner`: A request of length L has exactly ceil(L / 256) blocks, each (request, block) pair in exactly one slot, on the request's own instance or on a lending instance; other slots hold -1. For any two different instances i and j, at most 4 slots of i hold blocks of requests of j, and exactly 4 for some pair. The slot holds tokens block_index * 256 to block_index * 256 + 255 of its request; 0 in free slots.
All inputs are finite; a program needn't handle non-finite values.
Results may differ from a plain program's by a relative error of at most 0.022.
Values may be sent and summed in bfloat16 or wider, within the bound.
No kernel may reach another device: no remote copies, remote signals or barrier semaphores. Data moves between devices by JAX's collectives and lax.ppermute only.
A program may use at most 64 MiB of HBM per device.

v0:
```python
import jax
import jax.numpy as jnp
from jax import lax
from jax.sharding import PartitionSpec as P

masked_score = -1e30


def body(
    query, new_key, new_value, key_cache, value_cache, out_weight, lengths, block_owner, block_index
):
    req_local, heads_dev, head_dim = query.shape
    slot_count, block_len, kv_dev, _ = key_cache.shape
    per_kv = heads_dev // kv_dev
    total_req = lengths.shape[0]
    softmax_scale = head_dim ** (-0.5)
    in_use = block_owner >= 0
    holder = jnp.maximum(block_owner, 0)
    everyone = lax.all_gather(query, "inst", axis=0, tiled=True)
    picked = everyone[holder]
    grouped = picked.reshape(slot_count, kv_dev, per_kv, head_dim)
    scores = (
        jnp.einsum("pkgd,ptkd->pkgt", grouped, key_cache, preferred_element_type=jnp.float32)
        * softmax_scale
    )
    positions = block_index[:, None] * block_len + jnp.arange(block_len, dtype=jnp.int32)[None, :]
    usable = in_use[:, None] & (positions < lengths[holder][:, None])
    usable = usable[:, None, None, :]
    scores = jnp.where(usable, scores, masked_score)
    block_max = jnp.max(scores, axis=3)
    weights = jnp.where(usable, jnp.exp(scores - block_max[..., None]), 0.0).astype(jnp.bfloat16)
    block_sum = jnp.sum(weights.astype(jnp.float32), axis=3)
    block_out = jnp.einsum(
        "pkgt,ptkd->pkgd", weights, value_cache, preferred_element_type=jnp.float32
    )
    member = block_owner[:, None] == jnp.arange(total_req, dtype=jnp.int32)[None, :]
    local_max = jnp.max(
        jnp.where(member[:, :, None, None], block_max[:, None], masked_score), axis=0
    )
    rescale = jnp.exp(block_max - local_max[holder])
    onehot = member.astype(jnp.float32)
    local_sum = jnp.einsum(
        "pr,pkg->rkg", onehot, block_sum * rescale, precision=lax.Precision.HIGHEST
    )
    local_out = jnp.einsum(
        "pr,pkgd->rkgd", onehot, block_out * rescale[..., None], precision=lax.Precision.HIGHEST
    )
    global_max = lax.pmax(local_max, "inst")
    adjust = jnp.exp(local_max - global_max)
    merged_out, merged_sum = (
        lax.psum_scatter(
            (local_out * adjust[..., None]).astype(jnp.bfloat16),
            "inst",
            scatter_dimension=0,
            tiled=True,
        ).astype(jnp.float32),
        lax.psum_scatter(
            (local_sum * adjust).astype(jnp.bfloat16), "inst", scatter_dimension=0, tiled=True
        ).astype(jnp.float32),
    )
    own_max = lax.dynamic_slice_in_dim(global_max, lax.axis_index("inst") * req_local, req_local, 0)
    own_query = query.reshape(req_local, kv_dev, per_kv, head_dim)
    own_scores = (
        jnp.einsum("rkgd,rkd->rkg", own_query, new_key, preferred_element_type=jnp.float32)
        * softmax_scale
    )
    row_max = jnp.maximum(own_max, own_scores)
    carried = jnp.exp(own_max - row_max)
    own_weight = lax.optimization_barrier(
        jnp.exp(own_scores - row_max).astype(jnp.bfloat16)
    ).astype(jnp.float32)
    total_sum = merged_sum * carried + own_weight
    total_out = (
        merged_out * carried[..., None]
        + own_weight[..., None] * new_value.astype(jnp.float32)[:, :, None, :]
    )
    attended = (
        (total_out / total_sum[..., None])
        .astype(jnp.bfloat16)
        .reshape(req_local, heads_dev * head_dim)
    )
    partial_value = jnp.dot(attended, out_weight, preferred_element_type=jnp.float32)
    return lax.psum_scatter(
        partial_value.astype(jnp.bfloat16), "tp", scatter_dimension=1, tiled=True
    )


def solution(mesh):
    placed = (
        P("inst", "tp", None),
        P("inst", "tp", None),
        P("inst", "tp", None),
        P("inst", None, "tp", None),
        P("inst", None, "tp", None),
        P("tp", None),
        P(),
        P("inst"),
        P("inst"),
    )
    return jax.shard_map(
        body, mesh=mesh, in_specs=placed, out_specs=P("inst", "tp"), check_vma=False
    )
```

profile of v0, /device:TPU:32, one launch (start us, length us, event | category | flops | bytes accessed | tf_op | source)
XLA Modules:
  0.0 393.3 jit_solution(5166777595732980600)
XLA Ops:
  6.5 0.8 broadcast_maximum_fusion
  7.3 0.7 broadcast_compare_fusion
  8.0 0.7 iota_compare_fusion
  8.7 0.7 broadcast_multiply_fusion
  9.4 51.9 %all_gather.3 = bf16[256,8,128]{2,1,0:T(8,128)(2,1)S(1)} all-gather(bf16[8,8,128]{2,1,0:T(8,128)(2,1)} %param.9), channel_id=1, replica_groups=mesh['inst'=32,'tp'=8] {'inst'}, dimensions={0}, use_global_device_ids=true | all-gather | bytes 540672 | tf_op jit(solution)/shard_map/all_gather | solution.py:19
  61.3 1.4 gather_fusion
  62.7 0.6 gather_fusion.1
  63.2 0.1 fusion.18
  63.4 0.7 fusion.39
  64.1 0.1 select_reduce_fusion
  64.2 0.1 copy.40
  64.3 0.6 gather_fusion.2
  64.9 71.7 %pmax.7 = f32[256,1,8]{0,2,1:T(8,128)S(1)} all-reduce(f32[256,1,8]{0,2,1:T(8,128)S(1)} %bitcast.67), channel_id=1, replica_groups=mesh['inst'=32,'tp'=8] {'inst'}, use_global_device_ids=true, to_apply=%region_2.3 | all-reduce | flops 2048 | bytes 16384 | tf_op jit(solution)/shard_map/pmax | solution.py:48
  136.6 2.0 fusion.12
  138.7 0.0 copy-start.5
  138.7 0.7 fusion.5
  139.4 0.3 copy.55
  139.8 0.9 copy.65
  140.7 0.0 reduce-scatter.8.cloned.1.call-update
  140.7 0.0 reduce-scatter.6.cloned.1.call-start
  140.8 0.1 fusion.34
  140.9 0.1 copy.42
  141.0 0.1 fusion.33
  141.0 0.6 dynamic-slice
  142.3 0.2 convert_reduce_fusion
  142.5 0.2 fusion.16
  142.7 72.4 %all-reduce = bf16[256,1,8]{0,2,1:T(8,128)(2,1)S(1)} all-reduce(bf16[256,1,8]{0,2,1:T(8,128)(2,1)S(1)} %fusion.16), channel_id=3, replica_groups=mesh['inst'=32,'tp'=8] {'inst'}, use_global_device_ids=true, to_apply=%region_5.6.clone | all-reduce | flops 2048 | bytes 8192
  215.1 0.1 fusion.37
  215.2 133.9 %reduce-scatter.8.cloned.1.call-done = bf16[8,1024]{1,0:T(8,128)(2,1)} async-done(((bf16[256,1024]{1,0:T(8,128)(2,1)}), bf16[8,1024]{1,0:T(8,128)(2,1)}) %reduce-scatter.8.cloned.1.call-update) | async-done | bytes 16400
  349.1 5.3 %convolution_convert_fusion = bf16[8,4096]{1,0:T(8,128)(2,1)} fusion(bf16[1024,4096]{1,0:T(8,128)(2,1)} %param.14, bf16[8,1024]{1,0:T(8,128)(2,1)} %reduce-scatter.8.cloned.1.call-done, f32[8,8]{0,1:T(8,128)S(1)} %get-tuple-element.6, f32[8,128]{1,0:T(8,128)S(1)} %bitcast_convert_fusion, f32[8,8]{0,1:T(8,128)S(1)} %convert_bitcast_fusion, ...), kind=kOutput, calls=%fused_computation.3 | convolution fusion | flops 67190784 | bytes 8475392 | tf_op jit(solution)/shard_map/dot_general | solution.py:82
  354.4 0.0 reduce-scatter.6.cloned.1.call-update
  354.4 32.1 %reduce-scatter.6.cloned.1.call-done = bf16[8,512]{1,0:T(8,128)(2,1)} async-done(((bf16[8,4096]{1,0:T(8,128)(2,1)}), bf16[8,512]{1,0:T(8,128)(2,1)}) %reduce-scatter.6.cloned.1.call-update) | async-done | bytes 8208 | tf_op jit(solution)/shard_map/reduce_scatter | solution.py:83
  (18 shorter events, 0.1 us)
Async XLA Ops:
  6.5 56.8 %copy-start = (bf16[32,256,1,128]{3,1,2,0:T(8,128)(2,1)S(1)}, bf16[32,256,1,128]{3,1,2,0:T(8,128)(2,1)}, u32[]{:S(2)}) copy-start(bf16[32,256,1,128]{3,1,2,0:T(8,128)(2,1)} %param.12) | copy-start | bytes 6291460
  6.5 342.6 %reduce-scatter.8.cloned.1.call-start = ((), (), s32[]{:S(2)}) async-start(), calls=%async_computation.3 | async-start | bytes 540672
  63.3 75.3 %copy-start.2 = (s32[32]{0:T(128)S(1)}, s32[32]{0:T(128)}, u32[]{:S(2)}) copy-start(s32[32]{0:T(128)} %param.16) | copy-start | bytes 388
  138.6 2.1 copy-start.1
  138.7 2.1 copy-start.4
  138.7 2.4 copy-start.5
  138.7 76.4 %copy-start.3 = (bf16[8,1,128]{2,0,1:T(8,128)(2,1)S(1)}, bf16[8,1,128]{2,0,1:T(8,128)(2,1)}, u32[]{:S(2)}) copy-start(bf16[8,1,128]{2,0,1:T(8,128)(2,1)} %param.11) | copy-start | bytes 6148
  140.7 245.8 %reduce-scatter.6.cloned.1.call-start = ((), (), s32[]{:S(2)}) async-start(), calls=%async_computation.2 | async-start | bytes 73728 | tf_op jit(solution)/shard_map/reduce_scatter | solution.py:83
Sparse Core Ops, SparseCore 0:
  140.8 208.2 reduce-scatter.7
  354.5 31.8 reduce-scatter.5
where the time goes:
time: 394 us; the launch traced here: 393 us
  blocking collectives  196 us (50%)
  waiting for transfers between devices  166 us (42%)
  between operations  14.2 us (4%)
  matrix products  9.05 us (2%)
  local copies, waits for them, and re-layouts  4.62 us (1%)
    unnamed x3, waiting for transfers between devices  134 us
    unnamed x1, blocking collectives  72.4 us
    pmax x1, blocking collectives, body(): global_max = lax.pmax(local_max, 'inst')  71.7 us
    all_gather x1, blocking collectives, body(): everyone = lax.all_gather(query, 'inst', axis=0, tiled=True)  51.9 us
    reduce_scatter x1, waiting for transfers between devices, body(): lax.psum_scatter(partial_value.astype(jnp.bfloat16), 'tp', scatter_dimens...  32.1 us
  transfers between devices with their start and end apart: 2, of which 2 were waited for; matrix products, arithmetic and copies ran while one was open for 0% of the time, Pallas kernels for 0%

commit v1 on v0

v1 whole, which is shorter than its diff:
```python
import jax
import jax.numpy as jnp
from jax import lax
from jax.experimental import pallas as pl
from jax.experimental.pallas import tpu as pltpu
from jax.sharding import PartitionSpec as P

masked_score = -1e30
lent_slots = 4
f32 = jnp.float32
bf16 = jnp.bfloat16


def attend_kernel(
    owner_ref, index_ref, length_ref, query_ref, key_ref, value_ref,
    sent_ref, local_out_ref, local_note_ref, entry_out, entry_note, used_count,
):
    slots, block_len, head_dim = key_ref.shape
    heads = 8
    n_inst = query_ref.shape[0] // (8 * heads)
    spare = n_inst * lent_slots
    scale = head_dim ** (-0.5)
    me = lax.axis_index("inst")
    token = lax.broadcasted_iota(jnp.int32, (heads, block_len), 1)
    lane = lax.broadcasted_iota(jnp.int32, (heads, head_dim), 1)
    kind = lane % 4
    group = lane // 4
    blank = jnp.where(kind == 3, -1.0, 0.0).astype(f32)

    for e in range(spare):
        entry_out[e] = jnp.zeros((heads, head_dim), f32)
        entry_note[e] = blank
    for j in range(n_inst):
        used_count[j] = 0

    owners = [owner_ref[p] for p in range(slots)]
    holders = [jnp.maximum(o, 0) for o in owners]
    scores = []
    for p in range(slots):
        pair = query_ref[pl.ds(pl.multiple_of((holders[p] // 2) * 16, 16), 16), :]
        both = lax.dot_general(
            pair, key_ref[p], (((1,), (1,)), ((), ())), preferred_element_type=f32
        )
        scores.append(jnp.where(holders[p] % 2 == 1, both[heads:], both[:heads]) * scale)
    notes = []
    for p in range(slots):
        limit = jnp.where(
            owners[p] >= 0, length_ref[holders[p]] - index_ref[p] * block_len, 0
        )
        live = token < limit
        score = jnp.where(live, scores[p], masked_score)
        top = jnp.max(score, axis=1, keepdims=True)
        top = (top + jnp.abs(top) * 0.0078125).astype(bf16).astype(f32)
        weight = jnp.where(live, jnp.exp(score - top), 0.0).astype(bf16)
        total = jnp.sum(weight.astype(f32), axis=1, keepdims=True)
        out = jnp.dot(weight, value_ref[p], preferred_element_type=f32)
        home = holders[p] // 8
        request = (holders[p] % 8).astype(f32)
        foreign = (owners[p] >= 0) & (home != me)
        local = (owners[p] >= 0) & (home == me)
        rank = used_count[home]
        used_count[home] = rank + foreign.astype(jnp.int32)
        place = jnp.where(foreign, home * lent_slots + rank, spare)
        high = total.astype(bf16).astype(f32)
        note = jnp.where(kind == 0, top, jnp.where(kind == 1, high, total - high))
        entry_out[place] = out
        entry_note[place] = jnp.where(kind == 3, request, note)
        local_out_ref[p] = out
        notes.append(jnp.where(kind == 3, jnp.where(local, request, -1.0), note))
        if p % 4 == 3:
            a, b, c, d = notes[p - 3 : p + 1]
            local_note_ref[p // 4] = jnp.where(
                group == 0, a, jnp.where(group == 1, b, jnp.where(group == 2, c, d))
            )
    for jj in range(n_inst // 2):
        rows = []
        for j in (2 * jj, 2 * jj + 1):
            a, b, c, d = [entry_note[j * lent_slots + k] for k in range(lent_slots)]
            rows += [entry_out[j * lent_slots + k] for k in range(lent_slots)]
            rows.append(
                jnp.where(group == 0, a, jnp.where(group == 1, b, jnp.where(group == 2, c, d)))
            )
        sent_ref[pl.ds(80 * jj, 80), :] = jnp.concatenate(rows, axis=0).astype(bf16)


def merge_kernel(
    got_ref, local_out_ref, local_note_ref, query_ref, new_key_ref, new_value_ref, weight_ref,
    attended_ref, send_ref, attended_rows,
):
    requests = 8
    heads = 8
    head_dim = query_ref.shape[1]
    scale = head_dim ** (-0.5)
    groups = got_ref.shape[0] // 40 + local_note_ref.shape[0]
    outs, notes = [], []
    for jj in range(got_ref.shape[0] // 80):
        block = got_ref[pl.ds(80 * jj, 80), :].astype(f32)
        for j in range(2):
            rows = block[40 * j : 40 * (j + 1)]
            outs.append([rows[8 * k : 8 * k + 8] for k in range(lent_slots)])
            notes.append(rows[32:40])
    for g in range(local_note_ref.shape[0]):
        outs.append([local_out_ref[4 * g + k] for k in range(lent_slots)])
        notes.append(local_note_ref[g])
    note = jnp.concatenate(notes, axis=0)
    lane = lax.broadcasted_iota(jnp.int32, note.shape, 1)
    holds = (lane % 4 == 0) & (lane < 4 * lent_slots)
    sums = pltpu.roll(note, head_dim - 1, 1) + pltpu.roll(note, head_dim - 2, 1)
    who = jnp.where(holds, pltpu.roll(note, head_dim - 3, 1), -1.0)
    shape = (groups, heads, head_dim)
    note, sums, who = note.reshape(shape), sums.reshape(shape), who.reshape(shape)

    query = query_ref[...].astype(f32).reshape(requests, heads, head_dim)
    new_key = new_key_ref[...].astype(f32)
    new_value = new_value_ref[...].astype(f32)
    tops, own_scores = [], []
    chosen = jnp.zeros(shape, f32)
    for r in range(requests):
        own = jnp.sum(query[r] * new_key[r : r + 1], axis=1, keepdims=True) * scale
        mine = jnp.max(jnp.where(who == r, note, masked_score), axis=0)
        top = jnp.maximum(jnp.max(mine, axis=1, keepdims=True), own)
        chosen = jnp.where(who == r, top[None], chosen)
        tops.append(top)
        own_scores.append(own)
    factor = jnp.where(who >= 0, jnp.exp(note - chosen), 0.0)
    scaled = factor * sums
    totals, values = [], []
    for r in range(requests):
        own_weight = jnp.exp(own_scores[r] - tops[r]).astype(bf16).astype(f32)
        cached = jnp.sum(jnp.where(who == r, scaled, 0.0), axis=0)
        totals.append(jnp.sum(cached, axis=1, keepdims=True) + own_weight)
        values.append(own_weight * new_value[r : r + 1])
    for g in range(groups):
        for k in range(lent_slots):
            at = slice(4 * k, 4 * k + 1)
            part = factor[g][:, at] * outs[g][k]
            whose = jnp.broadcast_to(who[g][:, at], part.shape)
            for r in range(requests):
                values[r] = values[r] + jnp.where(whose == r, part, 0.0)
    for r in range(requests):
        attended_rows[r] = values[r] / totals[r]
    attended = jnp.concatenate([attended_rows[:, h, :] for h in range(heads)], axis=1).astype(bf16)
    attended_ref[...] = attended
    other = 1 - lax.axis_index("tp") % 2
    width = send_ref.shape[1] // 4
    for n in range(4):
        at = pl.ds(pl.multiple_of((2 * n + other) * width, width), width)
        send_ref[:, n * width : (n + 1) * width] = jnp.dot(
            attended, weight_ref[:, at], preferred_element_type=f32
        ).astype(bf16)


def project_kernel(attended_ref, weight_ref, keep_ref):
    mine = lax.axis_index("tp") % 2
    width = keep_ref.shape[1] // 4
    attended = attended_ref[...]
    for n in range(4):
        at = pl.ds(pl.multiple_of((2 * n + mine) * width, width), width)
        keep_ref[:, n * width : (n + 1) * width] = jnp.dot(
            attended, weight_ref[:, at], preferred_element_type=f32
        )


def split_kernel(keep_ref, got_ref, own_ref, *send_refs):
    chip = lax.axis_index("tp") // 2
    width = own_ref.shape[1]
    for k in range(4):
        at = pl.ds(pl.multiple_of(lax.rem(chip + k, 4) * width, width), width)
        total = keep_ref[:, at] + got_ref[:, at].astype(f32)
        if k == 0:
            own_ref[...] = total
        else:
            send_refs[k - 1][...] = total.astype(bf16)


def vmem(n):
    return [pl.BlockSpec(memory_space=pltpu.VMEM)] * n


def smem(n):
    return [pl.BlockSpec(memory_space=pltpu.SMEM)] * n


def body(
    query, new_key, new_value, key_cache, value_cache, out_weight, lengths, block_owner, block_index
):
    req_local, heads_dev, head_dim = query.shape
    slot_count, block_len, _, _ = key_cache.shape
    n_inst = lengths.shape[0] // req_local
    n_tp = lax.axis_size("tp")
    rows = req_local * heads_dev
    features = out_weight.shape[1]
    params = pltpu.CompilerParams(vmem_limit_bytes=40 * 1024 * 1024)
    shape = jax.ShapeDtypeStruct

    flat_query = query.reshape(rows, head_dim)
    copies = jnp.broadcast_to(flat_query[None], (n_inst, rows, head_dim))
    everyone = lax.all_to_all(copies, "inst", 0, 0, tiled=True)
    keys = key_cache.reshape(slot_count, block_len, head_dim)
    values = value_cache.reshape(slot_count, block_len, head_dim)
    sent_rows = (lent_slots + 1) * heads_dev
    sent, local_out, local_note = pl.pallas_call(
        attend_kernel,
        out_shape=(
            shape((n_inst * sent_rows, head_dim), bf16),
            shape((slot_count, heads_dev, head_dim), f32),
            shape((slot_count // lent_slots, heads_dev, head_dim), f32),
        ),
        in_specs=smem(3) + vmem(3),
        out_specs=tuple(vmem(3)),
        scratch_shapes=[
            pltpu.VMEM((n_inst * lent_slots + 1, heads_dev, head_dim), f32),
            pltpu.VMEM((n_inst * lent_slots + 1, heads_dev, head_dim), f32),
            pltpu.SMEM((n_inst,), jnp.int32),
        ],
        compiler_params=params,
        name="attend",
    )(block_owner, block_index, lengths, everyone.reshape(n_inst * rows, head_dim), keys, values)
    got = lax.all_to_all(
        sent.reshape(n_inst, sent_rows, head_dim), "inst", 0, 0, tiled=True
    ).reshape(n_inst * sent_rows, head_dim)
    attended, for_core = pl.pallas_call(
        merge_kernel,
        out_shape=(
            shape((req_local, heads_dev * head_dim), bf16),
            shape((req_local, features // 2), bf16),
        ),
        in_specs=vmem(7),
        out_specs=tuple(vmem(2)),
        scratch_shapes=[pltpu.VMEM((req_local, heads_dev, head_dim), f32)],
        compiler_params=params,
        name="merge",
    )(
        got, local_out, local_note, flat_query,
        new_key.reshape(req_local, head_dim), new_value.reshape(req_local, head_dim), out_weight,
    )
    from_core = lax.ppermute(for_core, "tp", [(i, i ^ 1) for i in range(n_tp)])
    keep = pl.pallas_call(
        project_kernel,
        out_shape=shape((req_local, features // 2), f32),
        in_specs=vmem(2),
        out_specs=vmem(1)[0],
        compiler_params=params,
        cost_estimate=pl.CostEstimate(
            flops=req_local * heads_dev * head_dim * features, bytes_accessed=4194304, transcendentals=0
        ),
        name="project",
    )(attended, out_weight)
    width = features // n_tp
    own, *parts = pl.pallas_call(
        split_kernel,
        out_shape=(shape((req_local, width), f32),) + (shape((req_local, width), bf16),) * 3,
        in_specs=vmem(2),
        out_specs=tuple(vmem(4)),
        compiler_params=params,
        name="split",
    )(keep, from_core)
    total = own
    for k in (1, 2, 3):
        pairs = [(i, (i + 2 * k) % n_tp) for i in range(n_tp)]
        total = total + lax.ppermute(parts[k - 1], "tp", pairs).astype(f32)
    return total.astype(bf16)


def solution(mesh):
    placed = (
        P("inst", "tp", None),
        P("inst", "tp", None),
        P("inst", "tp", None),
        P("inst", None, "tp", None),
        P("inst", None, "tp", None),
        P("tp", None),
        P(),
        P("inst"),
        P("inst"),
    )
    return jax.shard_map(
        body, mesh=mesh, in_specs=placed, out_specs=P("inst", "tp"), check_vma=False
    )
```

time: 394 us -> 70.4 us (0.18)
  waiting for transfers between devices: 166 us -> 2.22 us
  blocking collectives: 196 us -> 46.4 us
  between operations: 14.2 us -> 0.05 us
  matrix products: 9.05 us -> 0 us
  local copies, waits for them, and re-layouts: 4.62 us -> 10.9 us
  starting transfers between devices: 0.04 us -> 5.73 us
  Pallas kernels: 0 us -> 4.23 us
    unnamed x3 -> x0, waiting for transfers between devices: 134 us -> none
    unnamed x1 -> x0, blocking collectives: 72.4 us -> none
    pmax x1 -> x0, blocking collectives: 71.7 us -> none  [body(): global_max = lax.pmax(local_max, 'inst')]
    all_gather x1 -> x0, blocking collectives: 51.9 us -> none  [body(): everyone = lax.all_gather(query, 'inst', axis=0, tiled=True)]
    all_to_all x0 -> x2, blocking collectives: none -> 46.4 us  [the longest x1 28.8 us: body(): everyone = lax.all_to_all(copies, 'inst', 0, 0, tiled=True)]
    reduce_scatter x1 -> x0, waiting for transfers between devices: 32.1 us -> none  [body(): lax.psum_scatter(partial_value.astype(jnp.bfloat16), 'tp', scatter_dimens...]
    dot_general x6 -> x0, matrix products: 9.05 us -> none  [the longest x1 5.26 us: body(): jnp.dot(attended, out_weight, preferred_element_type=jnp.float32)]
    unnamed x15 -> x20, local copies, waits for them, and re-layouts: 1.86 us -> 10 us
  transfers between devices with their start and end apart: 2 -> 4, of which waited for: 2 -> 2; matrix products, arithmetic and copies ran while one was open for 0% -> 0% of each run, Pallas kernels for 0% -> 1%
where the time goes in v1:
time: 70.4 us; the launch traced here: 70 us
  blocking collectives  46.4 us (66%)
  local copies, waits for them, and re-layouts  10.9 us (15%)
  starting transfers between devices  5.73 us (8%)
  Pallas kernels  4.23 us (6%)
  waiting for transfers between devices  2.22 us (3%)
    all_to_all x1, blocking collectives, body(): everyone = lax.all_to_all(copies, 'inst', 0, 0, tiled=True)  28.8 us
    all_to_all x1, blocking collectives, body(): lax.all_to_all(sent.reshape(n_inst, sent_rows, head_dim), 'inst', 0, 0, t...  17.6 us
    unnamed x20, local copies, waits for them, and re-layouts  10 us
    ppermute x3, starting transfers between devices, body(): total = total + lax.ppermute(parts[k - 1], 'tp', pairs).astype(f32)  5.73 us
    ppermute x3, waiting for transfers between devices, body(): total = total + lax.ppermute(parts[k - 1], 'tp', pairs).astype(f32)  2.22 us
    pallas_call x1, Pallas kernels, body(): pl.pallas_call(merge_kernel, out_shape=(shape((req_local, heads_dev * hea...  1.91 us
    pallas_call x1, Pallas kernels, body(): pl.pallas_call(attend_kernel, out_shape=(shape((n_inst * sent_rows, head_...  1.65 us
  transfers between devices with their start and end apart: 4, of which 2 were waited for; matrix products, arithmetic and copies ran while one was open for 0% of the time, Pallas kernels for 1%

profile of v1, /device:TPU:32, one launch (start us, length us, event | category | flops | bytes accessed | tf_op | source)
XLA Modules:
  0.0 70.0 jit_solution(9902834062024797691)
XLA Ops:
  0.0 0.8 %broadcast_in_dim.8 = bf16[32,64,128]{2,1,0:T(8,128)(2,1)S(1)} broadcast(bf16[64,128]{1,0:T(8,128)(2,1)} %bitcast.13), dimensions={1,2} | broadcast | bytes 540672 | tf_op jit(solution)/shard_map/broadcast_in_dim | solution.py:197
  0.8 28.8 %all_to_all.10 = bf16[32,64,128]{2,1,0:T(8,128)(2,1)S(1)} all-to-all(bf16[32,64,128]{2,1,0:T(8,128)(2,1)S(1)} %broadcast_in_dim.8), channel_id=1, replica_groups=mesh['inst'=32,'tp'=8] {'inst'}, dimensions={0} | all-to-all | bytes 1048576 | tf_op jit(solution)/shard_map/all_to_all | solution.py:198
  29.6 0.0 copy-start.2
  29.6 1.6 %copy-done.2 = bf16[32,256,1,128]{3,1,2,0:T(8,128)(2,1)S(1)} copy-done((bf16[32,256,1,128]{3,1,2,0:T(8,128)(2,1)S(1)}, bf16[32,256,1,128]{3,1,2,0:T(8,128)(2,1)}, u32[]{:S(2)}) %copy-start.2) | copy-done | bytes 2097176
  31.2 0.0 copy-start.3
  31.2 1.6 %copy-done.3 = bf16[32,256,1,128]{3,1,2,0:T(8,128)(2,1)S(1)} copy-done((bf16[32,256,1,128]{3,1,2,0:T(8,128)(2,1)S(1)}, bf16[32,256,1,128]{3,1,2,0:T(8,128)(2,1)}, u32[]{:S(2)}) %copy-start.3) | copy-done | bytes 2097176
  32.8 0.0 copy-start.7
  32.8 0.7 copy-done.7
  33.5 0.0 copy-start.8
  33.5 0.7 copy-done.8
  34.1 0.0 copy-start.9
  34.1 0.7 copy-done.9
  34.8 0.0 copy-start.4
  34.8 1.6 %attend.1 = (bf16[1280,128]{1,0:T(8,128)(2,1)S(1)}, f32[32,8,128]{2,1,0:T(8,128)S(1)}, f32[8,8,128]{2,1,0:T(8,128)S(1)}) custom-call(s32[32]{0:T(128)S(1)} %copy-done.8, s32[32]{0:T(128)S(1)} %copy-done.9, s32[256]{0:T(256)S(1)} %copy-done.7, bf16[2048,128]{1,0:T(8,128)(2,1)S(1)} %bitcast.8, bf16[32,256,128]{2,1,0:T(8,128)(2,1)S(1)} %bitcast.9, ...), custom_call_target="tpu_custom_call" | custom-call | tf_op jit(solution)/shard_map/attend/pallas_call | solution.py:202
  36.4 17.6 %all_to_all.11 = bf16[32,40,128]{2,1,0:T(8,128)(2,1)S(1)} all-to-all(bf16[32,40,128]{2,1,0:T(8,128)(2,1)S(1)} %bitcast.12), channel_id=1, replica_groups=mesh['inst'=32,'tp'=8] {'inst'}, dimensions={0} | all-to-all | bytes 655360 | tf_op jit(solution)/shard_map/all_to_all | solution.py:219
  54.0 0.0 copy-done.4
  54.0 0.0 copy-done.5
  54.0 0.0 copy-done.6
  54.0 0.0 copy-start
  54.1 3.4 %copy-done = bf16[1024,4096]{1,0:T(8,128)(2,1)S(1)} copy-done((bf16[1024,4096]{1,0:T(8,128)(2,1)S(1)}, bf16[1024,4096]{1,0:T(8,128)(2,1)}, u32[]{:S(2)}) %copy-start) | copy-done | bytes 8388632
  57.4 1.9 %merge.1 = (bf16[8,1024]{1,0:T(8,128)(2,1)S(1)}, bf16[8,2048]{1,0:T(8,128)(2,1)S(1)}) custom-call(bf16[1280,128]{1,0:T(8,128)(2,1)S(1)} %bitcast.11, f32[32,8,128]{2,1,0:T(8,128)S(1)} %get-tuple-element.15.local_out_ref, f32[8,8,128]{2,1,0:T(8,128)S(1)} %get-tuple-element.16.local_note_ref, bf16[64,128]{1,0:T(8,128)(2,1)S(1)} %bitcast.14, ...), custom_call_target="tpu_custom_call" | custom-call | tf_op jit(solution)/shard_map/merge/pallas_call | solution.py:222
  59.3 0.0 collective-permute-start
  59.3 1.5 %copy-done.1 = bf16[1024,4096]{1,0:T(8,128)(2,1)S(1)} copy-done((bf16[1024,4096]{1,0:T(8,128)(2,1)S(1)}, bf16[1024,4096]{1,0:T(8,128)(2,1)}, u32[]{:S(2)}) %copy-start.1) | copy-done | bytes 8388632
  60.8 0.6 project.1.keep_ref
  61.5 0.0 collective-permute-done.got_ref
  61.5 1.6 %collective-permute-start.1 = (bf16[8,512]{1,0:T(8,128)(2,1)S(1)}, bf16[8,512]{1,0:T(8,128)(2,1)S(1)}, u32[]{:S(2)}, u32[]{:S(2)}) collective-permute-start(bf16[8,512]{1,0:T(8,128)(2,1)S(1)} %get-tuple-element.20), channel_id=1, source_target_pairs={{0,2},{1,3},{2,4},{3,5},{4,6},{5,7},{6,0},{7,1},{8,10},{9,11},{10,... | collective-permute-start | bytes 24584 | tf_op jit(solution)/shard_map/ppermute | solution.py:261
  63.1 2.7 %collective-permute-start.2 = (bf16[8,512]{1,0:T(8,128)(2,1)S(1)}, bf16[8,512]{1,0:T(8,128)(2,1)S(1)}, u32[]{:S(2)}, u32[]{:S(2)}) collective-permute-start(bf16[8,512]{1,0:T(8,128)(2,1)S(1)} %get-tuple-element.21), channel_id=1, source_target_pairs={{0,4},{1,5},{2,6},{3,7},{4,0},{5,1},{6,2},{7,3},{8,12},{9,13},{10,... | collective-permute-start | bytes 24584 | tf_op jit(solution)/shard_map/ppermute | solution.py:261
  65.8 1.4 %collective-permute-start.3 = (bf16[8,512]{1,0:T(8,128)(2,1)S(1)}, bf16[8,512]{1,0:T(8,128)(2,1)S(1)}, u32[]{:S(2)}, u32[]{:S(2)}) collective-permute-start(bf16[8,512]{1,0:T(8,128)(2,1)S(1)} %get-tuple-element.22), channel_id=1, source_target_pairs={{0,6},{1,7},{2,0},{3,1},{4,2},{5,3},{6,4},{7,5},{8,14},{9,15},{10,... | collective-permute-start | bytes 24584 | tf_op jit(solution)/shard_map/ppermute | solution.py:261
  67.2 0.0 collective-permute-done.1
  67.2 1.0 %collective-permute-done.2 = bf16[8,512]{1,0:T(8,128)(2,1)S(1)} collective-permute-done((bf16[8,512]{1,0:T(8,128)(2,1)S(1)}, bf16[8,512]{1,0:T(8,128)(2,1)S(1)}, u32[]{:S(2)}, u32[]{:S(2)}) %collective-permute-start.2) | collective-permute-done | bytes 8224 | tf_op jit(solution)/shard_map/ppermute | solution.py:261
  68.2 1.2 %collective-permute-done.3 = bf16[8,512]{1,0:T(8,128)(2,1)S(1)} collective-permute-done((bf16[8,512]{1,0:T(8,128)(2,1)S(1)}, bf16[8,512]{1,0:T(8,128)(2,1)S(1)}, u32[]{:S(2)}, u32[]{:S(2)}) %collective-permute-start.3) | collective-permute-done | bytes 8224 | tf_op jit(solution)/shard_map/ppermute | solution.py:261
  69.4 0.6 add_convert_fusion
  (4 shorter events, 0.0 us)
Async XLA Ops:
  29.6 1.6 %copy-start.2 = (bf16[32,256,1,128]{3,1,2,0:T(8,128)(2,1)S(1)}, bf16[32,256,1,128]{3,1,2,0:T(8,128)(2,1)}, u32[]{:S(2)}) copy-start(bf16[32,256,1,128]{3,1,2,0:T(8,128)(2,1)} %param.12) | copy-start | bytes 6291460
  31.2 1.6 %copy-start.3 = (bf16[32,256,1,128]{3,1,2,0:T(8,128)(2,1)S(1)}, bf16[32,256,1,128]{3,1,2,0:T(8,128)(2,1)}, u32[]{:S(2)}) copy-start(bf16[32,256,1,128]{3,1,2,0:T(8,128)(2,1)} %param.13) | copy-start | bytes 6291460
  32.8 0.7 copy-start.7
  33.5 0.7 copy-start.8
  34.1 0.7 copy-start.9
  34.8 19.2 %copy-start.4 = (bf16[8,8,128]{2,1,0:T(8,128)(2,1)S(1)}, bf16[8,8,128]{2,1,0:T(8,128)(2,1)}, u32[]{:S(2)}) copy-start(bf16[8,8,128]{2,1,0:T(8,128)(2,1)} %param.9) | copy-start | bytes 49156
  34.8 19.2 %copy-start.5 = (bf16[8,1,128]{2,0,1:T(8,128)(2,1)S(1)}, bf16[8,1,128]{2,0,1:T(8,128)(2,1)}, u32[]{:S(2)}) copy-start(bf16[8,1,128]{2,0,1:T(8,128)(2,1)} %param.10) | copy-start | bytes 6148
  34.8 19.2 %copy-start.6 = (bf16[8,1,128]{2,0,1:T(8,128)(2,1)S(1)}, bf16[8,1,128]{2,0,1:T(8,128)(2,1)}, u32[]{:S(2)}) copy-start(bf16[8,1,128]{2,0,1:T(8,128)(2,1)} %param.11) | copy-start | bytes 6148
  54.0 3.4 %copy-start = (bf16[1024,4096]{1,0:T(8,128)(2,1)S(1)}, bf16[1024,4096]{1,0:T(8,128)(2,1)}, u32[]{:S(2)}) copy-start(bf16[1024,4096]{1,0:T(8,128)(2,1)} %weight_ref.3) | copy-start | bytes 25165828
  57.4 3.4 %copy-start.1 = (bf16[1024,4096]{1,0:T(8,128)(2,1)S(1)}, bf16[1024,4096]{1,0:T(8,128)(2,1)}, u32[]{:S(2)}) copy-start(bf16[1024,4096]{1,0:T(8,128)(2,1)} %weight_ref.3) | copy-start | bytes 25165828
  59.3 2.1 %collective-permute-start = (bf16[8,2048]{1,0:T(8,128)(2,1)S(1)}, bf16[8,2048]{1,0:T(8,128)(2,1)S(1)}, u32[]{:S(2)}, u32[]{:S(2)}) collective-permute-start(bf16[8,2048]{1,0:T(8,128)(2,1)S(1)} %get-tuple-element.18), channel_id=1, source_target_pairs={{0,1},{1,0},{2,3},{3,2},{4,5},{5,4},{6,7},{7,6},{8,9},{9,8},{10,11... | collective-permute-start | bytes 98312 | tf_op jit(solution)/shard_map/ppermute | solution.py:237
  61.5 5.7 %collective-permute-start.1 = (bf16[8,512]{1,0:T(8,128)(2,1)S(1)}, bf16[8,512]{1,0:T(8,128)(2,1)S(1)}, u32[]{:S(2)}, u32[]{:S(2)}) collective-permute-start(bf16[8,512]{1,0:T(8,128)(2,1)S(1)} %get-tuple-element.20), channel_id=1, source_target_pairs={{0,2},{1,3},{2,4},{3,5},{4,6},{5,7},{6,0},{7,1},{8,10},{9,11},{10,... | collective-permute-start | bytes 24584 | tf_op jit(solution)/shard_map/ppermute | solution.py:261
  63.1 5.2 %collective-permute-start.2 = (bf16[8,512]{1,0:T(8,128)(2,1)S(1)}, bf16[8,512]{1,0:T(8,128)(2,1)S(1)}, u32[]{:S(2)}, u32[]{:S(2)}) collective-permute-start(bf16[8,512]{1,0:T(8,128)(2,1)S(1)} %get-tuple-element.21), channel_id=1, source_target_pairs={{0,4},{1,5},{2,6},{3,7},{4,0},{5,1},{6,2},{7,3},{8,12},{9,13},{10,... | collective-permute-start | bytes 24584 | tf_op jit(solution)/shard_map/ppermute | solution.py:261
  65.8 3.7 %collective-permute-start.3 = (bf16[8,512]{1,0:T(8,128)(2,1)S(1)}, bf16[8,512]{1,0:T(8,128)(2,1)S(1)}, u32[]{:S(2)}, u32[]{:S(2)}) collective-permute-start(bf16[8,512]{1,0:T(8,128)(2,1)S(1)} %get-tuple-element.22), channel_id=1, source_target_pairs={{0,6},{1,7},{2,0},{3,1},{4,2},{5,3},{6,4},{7,5},{8,14},{9,15},{10,... | collective-permute-start | bytes 24584 | tf_op jit(solution)/shard_map/ppermute | solution.py:261

commit v2 on v1

--- a/solution.py
+++ b/solution.py
@@ -9,6 +9,11 @@
 lent_slots = 4
 f32 = jnp.float32
 bf16 = jnp.bfloat16
+
+
+def copies_kernel(query_ref, copies_ref):
+    for j in range(copies_ref.shape[0]):
+        copies_ref[j] = query_ref[...]
 
 
 def attend_kernel(
@@ -85,7 +90,7 @@
 
 def merge_kernel(
     got_ref, local_out_ref, local_note_ref, query_ref, new_key_ref, new_value_ref, weight_ref,
-    attended_ref, send_ref, attended_rows,
+    send_ref, keep_ref, attended_rows,
 ):
     requests = 8
     heads = 8
@@ -140,7 +145,6 @@
     for r in range(requests):
         attended_rows[r] = values[r] / totals[r]
     attended = jnp.concatenate([attended_rows[:, h, :] for h in range(heads)], axis=1).astype(bf16)
-    attended_ref[...] = attended
     other = 1 - lax.axis_index("tp") % 2
     width = send_ref.shape[1] // 4
     for n in range(4):
@@ -148,14 +152,7 @@
         send_ref[:, n * width : (n + 1) * width] = jnp.dot(
             attended, weight_ref[:, at], preferred_element_type=f32
         ).astype(bf16)
-
-
-def project_kernel(attended_ref, weight_ref, keep_ref):
-    mine = lax.axis_index("tp") % 2
-    width = keep_ref.shape[1] // 4
-    attended = attended_ref[...]
-    for n in range(4):
-        at = pl.ds(pl.multiple_of((2 * n + mine) * width, width), width)
+        at = pl.ds(pl.multiple_of((2 * n + 1 - other) * width, width), width)
         keep_ref[:, n * width : (n + 1) * width] = jnp.dot(
             attended, weight_ref[:, at], preferred_element_type=f32
         )
@@ -190,11 +187,19 @@
     n_tp = lax.axis_size("tp")
     rows = req_local * heads_dev
     features = out_weight.shape[1]
-    params = pltpu.CompilerParams(vmem_limit_bytes=40 * 1024 * 1024)
+    params = pltpu.CompilerParams(vmem_limit_bytes=24 * 1024 * 1024)
     shape = jax.ShapeDtypeStruct
 
     flat_query = query.reshape(rows, head_dim)
-    copies = jnp.broadcast_to(flat_query[None], (n_inst, rows, head_dim))
+    copies = pl.pallas_call(
+        copies_kernel,
+        out_shape=shape((n_inst, rows, head_dim), bf16),
+        in_specs=vmem(1),
+        out_specs=vmem(1)[0],
+        compiler_params=params,
+        cost_estimate=pl.CostEstimate(flops=20_000_000_000, bytes_accessed=1_000_000, transcendentals=0),
+        name="copies",
+    )(flat_query)
     everyone = lax.all_to_all(copies, "inst", 0, 0, tiled=True)
     keys = key_cache.reshape(slot_count, block_len, head_dim)
     values = value_cache.reshape(slot_count, block_len, head_dim)
@@ -219,11 +224,11 @@
     got = lax.all_to_all(
         sent.reshape(n_inst, sent_rows, head_dim), "inst", 0, 0, tiled=True
     ).reshape(n_inst * sent_rows, head_dim)
-    attended, for_core = pl.pallas_call(
+    for_core, keep = pl.pallas_call(
         merge_kernel,
         out_shape=(
-            shape((req_local, heads_dev * head_dim), bf16),
             shape((req_local, features // 2), bf16),
+            shape((req_local, features // 2), f32),
         ),
         in_specs=vmem(7),
         out_specs=tuple(vmem(2)),
@@ -235,17 +240,6 @@
         new_key.reshape(req_local, head_dim), new_value.reshape(req_local, head_dim), out_weight,
     )
     from_core = lax.ppermute(for_core, "tp", [(i, i ^ 1) for i in range(n_tp)])
-    keep = pl.pallas_call(
-        project_kernel,
-        out_shape=shape((req_local, features // 2), f32),
-        in_specs=vmem(2),
-        out_specs=vmem(1)[0],
-        compiler_params=params,
-        cost_estimate=pl.CostEstimate(
-            flops=req_local * heads_dev * head_dim * features, bytes_accessed=4194304, transcendentals=0
-        ),
-        name="project",
-    )(attended, out_weight)
     width = features // n_tp
     own, *parts = pl.pallas_call(
         split_kernel,

time: 70.4 us -> 61.8 us (0.88)
  local copies, waits for them, and re-layouts: 10.9 us -> 0.91 us
  waiting for transfers between devices: 2.22 us -> 3.43 us
    unnamed x20 -> x22, local copies, waits for them, and re-layouts: 10 us -> 0.91 us
    ppermute x1, waiting for transfers between devices: 0.01 us -> 1.21 us  [body(): from_core = lax.ppermute(for_core, 'tp', [(i, i ^ 1) for i in range(n_tp)])]
    broadcast_in_dim x1 -> x0, local copies, waits for them, and re-layouts: 0.82 us -> none  [body(): copies = jnp.broadcast_to(flat_query[None], (n_inst, rows, head_dim))]
  transfers between devices with their start and end apart: 4 -> 4, of which waited for: 2 -> 3; matrix products, arithmetic and copies ran while one was open for 0% -> 0% of each run, Pallas kernels for 1% -> 0%
where the time goes in v2:
time: 61.8 us; the launch traced here: 61.6 us
  blocking collectives  46.6 us (75%)
  starting transfers between devices  5.73 us (9%)
  Pallas kernels  4.19 us (7%)
  waiting for transfers between devices  3.43 us (6%)
  local copies, waits for them, and re-layouts  0.91 us (1%)
    all_to_all x1, blocking collectives, body(): everyone = lax.all_to_all(copies, 'inst', 0, 0, tiled=True)  29 us
    all_to_all x1, blocking collectives, body(): lax.all_to_all(sent.reshape(n_inst, sent_rows, head_dim), 'inst', 0, 0, t...  17.6 us
    ppermute x3, starting transfers between devices, body(): total = total + lax.ppermute(parts[k - 1], 'tp', pairs).astype(f32)  5.73 us
    pallas_call x1, Pallas kernels, body(): pl.pallas_call(merge_kernel, out_shape=(shape((req_local, features // 2),...  2.46 us
    ppermute x3, waiting for transfers between devices, body(): total = total + lax.ppermute(parts[k - 1], 'tp', pairs).astype(f32)  2.22 us
    pallas_call x1, Pallas kernels, body(): pl.pallas_call(attend_kernel, out_shape=(shape((n_inst * sent_rows, head_...  1.64 us
  transfers between devices with their start and end apart: 4, of which 3 were waited for; matrix products, arithmetic and copies ran while one was open for 0% of the time, Pallas kernels for 0%

profile of v2, /device:TPU:32, one launch (start us, length us, event | category | flops | bytes accessed | tf_op | source)
XLA Modules:
  0.0 61.6 jit_solution(16117720670076489428)
XLA Ops:
  0.0 0.0 slice-start
  0.0 0.0 copy-start.2
  0.0 0.9 %copy-done.2 = bf16[8,8,128]{2,1,0:T(8,128)(2,1)S(1)} copy-done((bf16[8,8,128]{2,1,0:T(8,128)(2,1)S(1)}, bf16[8,8,128]{2,1,0:T(8,128)(2,1)}, u32[]{:S(2)}) %copy-start.2) | copy-done | bytes 16408
  0.9 0.0 copy-start.8
  0.9 0.0 slice-start.1
  0.9 0.1 copies.1
  1.0 29.0 %all_to_all.10 = bf16[32,64,128]{2,1,0:T(8,128)(2,1)S(1)} all-to-all(bf16[32,64,128]{2,1,0:T(8,128)(2,1)S(1)} %copies.1), channel_id=1, replica_groups=mesh['inst'=32,'tp'=8] {'inst'}, dimensions={0} | all-to-all | bytes 1048576 | tf_op jit(solution)/shard_map/all_to_all | solution.py:203
  30.0 0.0 copy-done
  30.0 0.0 copy-done.1
  30.0 0.0 copy-done.6
  30.0 0.0 copy-done.7
  30.0 0.0 copy-done.8
  30.0 0.0 copy-start.3
  30.1 0.0 copy-start.4
  30.1 0.0 copy-start.5
  30.1 1.6 %attend.1 = (bf16[1280,128]{1,0:T(8,128)(2,1)S(1)}, f32[32,8,128]{2,1,0:T(8,128)S(1)}, f32[8,8,128]{2,1,0:T(8,128)S(1)}) custom-call(s32[32]{0:T(128)S(1)} %copy-done.7, s32[32]{0:T(128)S(1)} %copy-done.8, s32[256]{0:T(256)S(1)} %copy-done.6, bf16[2048,128]{1,0:T(8,128)(2,1)S(1)} %bitcast.10, bf16[32,256,128]{2,1,0:T(8,128)(2,1)S(1)} %bitcast.11, ...), custom_call_target="tpu_custom_call" | custom-call | tf_op jit(solution)/shard_map/attend/pallas_call | solution.py:207
  31.7 17.6 %all_to_all.11 = bf16[32,40,128]{2,1,0:T(8,128)(2,1)S(1)} all-to-all(bf16[32,40,128]{2,1,0:T(8,128)(2,1)S(1)} %bitcast.14), channel_id=1, replica_groups=mesh['inst'=32,'tp'=8] {'inst'}, dimensions={0} | all-to-all | bytes 655360 | tf_op jit(solution)/shard_map/all_to_all | solution.py:224
  49.3 0.0 slice-done
  49.3 0.0 slice-done.1
  49.3 0.0 copy-done.3
  49.3 0.0 copy-done.4
  49.3 0.0 copy-done.5
  49.4 2.5 %merge.1 = (bf16[8,2048]{1,0:T(8,128)(2,1)S(1)}, f32[8,2048]{1,0:T(8,128)S(1)}) custom-call(bf16[1280,128]{1,0:T(8,128)(2,1)S(1)} %bitcast.13, f32[32,8,128]{2,1,0:T(8,128)S(1)} %get-tuple-element.15.local_out_ref, f32[8,8,128]{2,1,0:T(8,128)S(1)} %get-tuple-element.16.local_note_ref, bf16[64,128]{1,0:T(8,128)(2,1)S(1)} %bitcast.16, ...), custom_call_target="tpu_custom_call" | custom-call | tf_op jit(solution)/shard_map/merge/pallas_call | solution.py:227
  51.8 0.0 collective-permute-start
  51.8 1.2 %collective-permute-done.got_ref = bf16[8,2048]{1,0:T(8,128)(2,1)S(1)} collective-permute-done((bf16[8,2048]{1,0:T(8,128)(2,1)S(1)}, bf16[8,2048]{1,0:T(8,128)(2,1)S(1)}, u32[]{:S(2)}, u32[]{:S(2)}) %collective-permute-start) | collective-permute-done | bytes 32800 | tf_op jit(solution)/shard_map/ppermute | solution.py:242
  53.1 1.6 %collective-permute-start.1 = (bf16[8,512]{1,0:T(8,128)(2,1)S(1)}, bf16[8,512]{1,0:T(8,128)(2,1)S(1)}, u32[]{:S(2)}, u32[]{:S(2)}) collective-permute-start(bf16[8,512]{1,0:T(8,128)(2,1)S(1)} %get-tuple-element.20), channel_id=1, source_target_pairs={{0,2},{1,3},{2,4},{3,5},{4,6},{5,7},{6,0},{7,1},{8,10},{9,11},{10,... | collective-permute-start | bytes 24584 | tf_op jit(solution)/shard_map/ppermute | solution.py:255
  54.6 2.7 %collective-permute-start.2 = (bf16[8,512]{1,0:T(8,128)(2,1)S(1)}, bf16[8,512]{1,0:T(8,128)(2,1)S(1)}, u32[]{:S(2)}, u32[]{:S(2)}) collective-permute-start(bf16[8,512]{1,0:T(8,128)(2,1)S(1)} %get-tuple-element.21), channel_id=1, source_target_pairs={{0,4},{1,5},{2,6},{3,7},{4,0},{5,1},{6,2},{7,3},{8,12},{9,13},{10,... | collective-permute-start | bytes 24584 | tf_op jit(solution)/shard_map/ppermute | solution.py:255
  57.3 1.4 %collective-permute-start.3 = (bf16[8,512]{1,0:T(8,128)(2,1)S(1)}, bf16[8,512]{1,0:T(8,128)(2,1)S(1)}, u32[]{:S(2)}, u32[]{:S(2)}) collective-permute-start(bf16[8,512]{1,0:T(8,128)(2,1)S(1)} %get-tuple-element.22), channel_id=1, source_target_pairs={{0,6},{1,7},{2,0},{3,1},{4,2},{5,3},{6,4},{7,5},{8,14},{9,15},{10,... | collective-permute-start | bytes 24584 | tf_op jit(solution)/shard_map/ppermute | solution.py:255
  58.8 0.0 collective-permute-done.1
  58.8 1.0 %collective-permute-done.2 = bf16[8,512]{1,0:T(8,128)(2,1)S(1)} collective-permute-done((bf16[8,512]{1,0:T(8,128)(2,1)S(1)}, bf16[8,512]{1,0:T(8,128)(2,1)S(1)}, u32[]{:S(2)}, u32[]{:S(2)}) %collective-permute-start.2) | collective-permute-done | bytes 8224 | tf_op jit(solution)/shard_map/ppermute | solution.py:255
  59.8 1.2 %collective-permute-done.3 = bf16[8,512]{1,0:T(8,128)(2,1)S(1)} collective-permute-done((bf16[8,512]{1,0:T(8,128)(2,1)S(1)}, bf16[8,512]{1,0:T(8,128)(2,1)S(1)}, u32[]{:S(2)}, u32[]{:S(2)}) %collective-permute-start.3) | collective-permute-done | bytes 8224 | tf_op jit(solution)/shard_map/ppermute | solution.py:255
  61.0 0.6 add_convert_fusion
  (6 shorter events, 0.0 us)
Async XLA Ops:
  0.0 49.3 %slice-start = ((s8[8388608]{0:T(1024)(128)(4,1)}), s8[4194304]{0:T(1024)(128)(4,1)S(1)}, s32[]{:S(2)}) async-start(s8[8388608]{0:T(1024)(128)(4,1)} %bitcast.8), calls=%async_computation.2 | async-start | bytes 8388608
  0.0 0.9 %copy-start.2 = (bf16[8,8,128]{2,1,0:T(8,128)(2,1)S(1)}, bf16[8,8,128]{2,1,0:T(8,128)(2,1)}, u32[]{:S(2)}) copy-start(bf16[8,8,128]{2,1,0:T(8,128)(2,1)} %param.9) | copy-start | bytes 49156
  0.9 29.1 %copy-start = (bf16[32,256,1,128]{3,1,2,0:T(8,128)(2,1)S(1)}, bf16[32,256,1,128]{3,1,2,0:T(8,128)(2,1)}, u32[]{:S(2)}) copy-start(bf16[32,256,1,128]{3,1,2,0:T(8,128)(2,1)} %param.12) | copy-start | bytes 6291460
  0.9 29.1 %copy-start.1 = (bf16[32,256,1,128]{3,1,2,0:T(8,128)(2,1)S(1)}, bf16[32,256,1,128]{3,1,2,0:T(8,128)(2,1)}, u32[]{:S(2)}) copy-start(bf16[32,256,1,128]{3,1,2,0:T(8,128)(2,1)} %param.13) | copy-start | bytes 6291460
  0.9 29.1 %copy-start.6 = (s32[256]{0:T(256)S(1)}, s32[256]{0:T(256)}, u32[]{:S(2)}) copy-start(s32[256]{0:T(256)} %length_ref.1) | copy-start | bytes 3076
  0.9 29.2 %copy-start.7 = (s32[32]{0:T(128)S(1)}, s32[32]{0:T(128)}, u32[]{:S(2)}) copy-start(s32[32]{0:T(128)} %owner_ref.1) | copy-start | bytes 388
  0.9 29.2 %copy-start.8 = (s32[32]{0:T(128)S(1)}, s32[32]{0:T(128)}, u32[]{:S(2)}) copy-start(s32[32]{0:T(128)} %index_ref.1) | copy-start | bytes 388
  0.9 48.4 %slice-start.1 = ((s8[8388608]{0:T(1024)(128)(4,1)}), s8[4194304]{0:T(1024)(128)(4,1)S(1)}, s32[]{:S(2)}) async-start(s8[8388608]{0:T(1024)(128)(4,1)} %bitcast.8), calls=%async_computation.3 | async-start | bytes 8388608
  30.0 19.3 %copy-start.3 = (bf16[8,8,128]{2,1,0:T(8,128)(2,1)S(1)}, bf16[8,8,128]{2,1,0:T(8,128)(2,1)}, u32[]{:S(2)}) copy-start(bf16[8,8,128]{2,1,0:T(8,128)(2,1)} %param.9) | copy-start | bytes 49156
  30.1 19.3 %copy-start.4 = (bf16[8,1,128]{2,0,1:T(8,128)(2,1)S(1)}, bf16[8,1,128]{2,0,1:T(8,128)(2,1)}, u32[]{:S(2)}) copy-start(bf16[8,1,128]{2,0,1:T(8,128)(2,1)} %param.10) | copy-start | bytes 6148
  30.1 19.3 %copy-start.5 = (bf16[8,1,128]{2,0,1:T(8,128)(2,1)S(1)}, bf16[8,1,128]{2,0,1:T(8,128)(2,1)}, u32[]{:S(2)}) copy-start(bf16[8,1,128]{2,0,1:T(8,128)(2,1)} %param.11) | copy-start | bytes 6148
  51.8 1.2 %collective-permute-start = (bf16[8,2048]{1,0:T(8,128)(2,1)S(1)}, bf16[8,2048]{1,0:T(8,128)(2,1)S(1)}, u32[]{:S(2)}, u32[]{:S(2)}) collective-permute-start(bf16[8,2048]{1,0:T(8,128)(2,1)S(1)} %get-tuple-element.18), channel_id=1, source_target_pairs={{0,1},{1,0},{2,3},{3,2},{4,5},{5,4},{6,7},{7,6},{8,9},{9,8},{10,11... | collective-permute-start | bytes 98312 | tf_op jit(solution)/shard_map/ppermute | solution.py:242
  53.1 5.7 %collective-permute-start.1 = (bf16[8,512]{1,0:T(8,128)(2,1)S(1)}, bf16[8,512]{1,0:T(8,128)(2,1)S(1)}, u32[]{:S(2)}, u32[]{:S(2)}) collective-permute-start(bf16[8,512]{1,0:T(8,128)(2,1)S(1)} %get-tuple-element.20), channel_id=1, source_target_pairs={{0,2},{1,3},{2,4},{3,5},{4,6},{5,7},{6,0},{7,1},{8,10},{9,11},{10,... | collective-permute-start | bytes 24584 | tf_op jit(solution)/shard_map/ppermute | solution.py:255
  54.6 5.2 %collective-permute-start.2 = (bf16[8,512]{1,0:T(8,128)(2,1)S(1)}, bf16[8,512]{1,0:T(8,128)(2,1)S(1)}, u32[]{:S(2)}, u32[]{:S(2)}) collective-permute-start(bf16[8,512]{1,0:T(8,128)(2,1)S(1)} %get-tuple-element.21), channel_id=1, source_target_pairs={{0,4},{1,5},{2,6},{3,7},{4,0},{5,1},{6,2},{7,3},{8,12},{9,13},{10,... | collective-permute-start | bytes 24584 | tf_op jit(solution)/shard_map/ppermute | solution.py:255
  57.3 3.7 %collective-permute-start.3 = (bf16[8,512]{1,0:T(8,128)(2,1)S(1)}, bf16[8,512]{1,0:T(8,128)(2,1)S(1)}, u32[]{:S(2)}, u32[]{:S(2)}) collective-permute-start(bf16[8,512]{1,0:T(8,128)(2,1)S(1)} %get-tuple-element.22), channel_id=1, source_target_pairs={{0,6},{1,7},{2,0},{3,1},{4,2},{5,3},{6,4},{7,5},{8,14},{9,15},{10,... | collective-permute-start | bytes 24584 | tf_op jit(solution)/shard_map/ppermute | solution.py:255

commit v3 on v1

--- a/solution.py
+++ b/solution.py
@@ -3,24 +3,35 @@
 from jax import lax
 from jax.experimental import pallas as pl
 from jax.experimental.pallas import tpu as pltpu
+from jax.sharding import Mesh
 from jax.sharding import PartitionSpec as P
 
 masked_score = -1e30
 lent_slots = 4
+inst = ("y", "z")
+ring_y = 4
 f32 = jnp.float32
 bf16 = jnp.bfloat16
 
 
+def copies_kernel(query_ref, copies_ref):
+    for j in range(copies_ref.shape[0]):
+        copies_ref[j] = query_ref[...]
+
+
 def attend_kernel(
-    owner_ref, index_ref, length_ref, query_ref, key_ref, value_ref,
+    owner_ref, index_ref, length_ref, row0_ref, row1_ref, row2_ref, row3_ref, key_ref, value_ref,
     sent_ref, local_out_ref, local_note_ref, entry_out, entry_note, used_count,
 ):
     slots, block_len, head_dim = key_ref.shape
     heads = 8
-    n_inst = query_ref.shape[0] // (8 * heads)
+    row_refs = (row0_ref, row1_ref, row2_ref, row3_ref)
+    row_requests = row0_ref.shape[0] // heads
+    n_inst = ring_y * row_requests // 8
     spare = n_inst * lent_slots
     scale = head_dim ** (-0.5)
-    me = lax.axis_index("inst")
+    my_row = lax.axis_index("y")
+    me = lax.axis_index(inst)
     token = lax.broadcasted_iota(jnp.int32, (heads, block_len), 1)
     lane = lax.broadcasted_iota(jnp.int32, (heads, head_dim), 1)
     kind = lane % 4
@@ -37,7 +48,11 @@
     holders = [jnp.maximum(o, 0) for o in owners]
     scores = []
     for p in range(slots):
-        pair = query_ref[pl.ds(pl.multiple_of((holders[p] // 2) * 16, 16), 16), :]
+        back = lax.rem(my_row + ring_y - holders[p] // row_requests, ring_y)
+        at = pl.ds(pl.multiple_of((lax.rem(holders[p], row_requests) // 2) * 16, 16), 16)
+        pair = row_refs[0][at, :]
+        for k in range(1, ring_y):
+            pair = jnp.where(back == k, row_refs[k][at, :], pair)
         both = lax.dot_general(
             pair, key_ref[p], (((1,), (1,)), ((), ())), preferred_element_type=f32
         )
@@ -87,58 +102,51 @@
     got_ref, local_out_ref, local_note_ref, query_ref, new_key_ref, new_value_ref, weight_ref,
     attended_ref, send_ref, attended_rows,
 ):
-    requests = 8
     heads = 8
-    head_dim = query_ref.shape[1]
+    rows, head_dim = query_ref.shape
+    requests = rows // heads
     scale = head_dim ** (-0.5)
-    groups = got_ref.shape[0] // 40 + local_note_ref.shape[0]
     outs, notes = [], []
     for jj in range(got_ref.shape[0] // 80):
         block = got_ref[pl.ds(80 * jj, 80), :].astype(f32)
-        for j in range(2):
-            rows = block[40 * j : 40 * (j + 1)]
-            outs.append([rows[8 * k : 8 * k + 8] for k in range(lent_slots)])
-            notes.append(rows[32:40])
+        for start in (0, 40):
+            outs.append([block[start + 8 * k : start + 8 * k + 8] for k in range(lent_slots)])
+            notes.append(block[start + 32 : start + 40])
     for g in range(local_note_ref.shape[0]):
         outs.append([local_out_ref[4 * g + k] for k in range(lent_slots)])
         notes.append(local_note_ref[g])
-    note = jnp.concatenate(notes, axis=0)
-    lane = lax.broadcasted_iota(jnp.int32, note.shape, 1)
-    holds = (lane % 4 == 0) & (lane < 4 * lent_slots)
-    sums = pltpu.roll(note, head_dim - 1, 1) + pltpu.roll(note, head_dim - 2, 1)
-    who = jnp.where(holds, pltpu.roll(note, head_dim - 3, 1), -1.0)
-    shape = (groups, heads, head_dim)
-    note, sums, who = note.reshape(shape), sums.reshape(shape), who.reshape(shape)
-
-    query = query_ref[...].astype(f32).reshape(requests, heads, head_dim)
-    new_key = new_key_ref[...].astype(f32)
-    new_value = new_value_ref[...].astype(f32)
-    tops, own_scores = [], []
-    chosen = jnp.zeros(shape, f32)
-    for r in range(requests):
-        own = jnp.sum(query[r] * new_key[r : r + 1], axis=1, keepdims=True) * scale
-        mine = jnp.max(jnp.where(who == r, note, masked_score), axis=0)
-        top = jnp.maximum(jnp.max(mine, axis=1, keepdims=True), own)
-        chosen = jnp.where(who == r, top[None], chosen)
-        tops.append(top)
-        own_scores.append(own)
-    factor = jnp.where(who >= 0, jnp.exp(note - chosen), 0.0)
-    scaled = factor * sums
-    totals, values = [], []
-    for r in range(requests):
-        own_weight = jnp.exp(own_scores[r] - tops[r]).astype(bf16).astype(f32)
-        cached = jnp.sum(jnp.where(who == r, scaled, 0.0), axis=0)
-        totals.append(jnp.sum(cached, axis=1, keepdims=True) + own_weight)
-        values.append(own_weight * new_value[r : r + 1])
-    for g in range(groups):
-        for k in range(lent_slots):
-            at = slice(4 * k, 4 * k + 1)
-            part = factor[g][:, at] * outs[g][k]
-            whose = jnp.broadcast_to(who[g][:, at], part.shape)
-            for r in range(requests):
-                values[r] = values[r] + jnp.where(whose == r, part, 0.0)
-    for r in range(requests):
-        attended_rows[r] = values[r] / totals[r]
+    while len(notes) % 16:
+        outs.append([jnp.zeros((heads, head_dim), f32)] * lent_slots)
+        notes.append(jnp.full((heads, head_dim), -1.0, f32))
+    turned = jnp.concatenate(
+        [jnp.concatenate(notes[g : g + 16], axis=0).T[:16] for g in range(0, len(notes), 16)], axis=1
+    )
+    entries = turned.shape[1]
+    head_of = lax.broadcasted_iota(jnp.int32, (1, entries), 1) % heads
+    row_id = lax.broadcasted_iota(jnp.int32, (rows, entries), 0).astype(f32)
+
+    spread = (requests, heads, head_dim)
+    new_key = jnp.broadcast_to(new_key_ref[...].astype(f32)[:, None, :], spread).reshape(rows, head_dim)
+    new_value = jnp.broadcast_to(new_value_ref[...].astype(f32)[:, None, :], spread).reshape(rows, head_dim)
+    own = jnp.sum(query_ref[...].astype(f32) * new_key, axis=1, keepdims=True) * scale
+
+    tops = []
+    for k in range(lent_slots):
+        whose = turned[4 * k + 3 : 4 * k + 4] * heads + head_of.astype(f32)
+        tops.append(jnp.where(row_id == whose, turned[4 * k : 4 * k + 1], masked_score))
+    most = jnp.maximum(jnp.maximum(tops[0], tops[1]), jnp.maximum(tops[2], tops[3]))
+    top = jnp.maximum(jnp.max(most, axis=1, keepdims=True), own)
+    own_weight = jnp.exp(own - top).astype(bf16).astype(f32)
+    total = 0.0
+    value = own_weight * new_value
+    for k in range(lent_slots):
+        factor = jnp.exp(tops[k] - top).astype(bf16)
+        sums = turned[4 * k + 1 : 4 * k + 2] + turned[4 * k + 2 : 4 * k + 3]
+        total = total + factor.astype(f32) * sums
+        part = jnp.concatenate([out[k] for out in outs], axis=0).astype(bf16)
+        value = value + jnp.dot(factor, part, preferred_element_type=f32)
+    total = jnp.sum(total, axis=1, keepdims=True) + own_weight
+    attended_rows[...] = (value / total).reshape(spread)
     attended = jnp.concatenate([attended_rows[:, h, :] for h in range(heads)], axis=1).astype(bf16)
     attended_ref[...] = attended
     other = 1 - lax.axis_index("tp") % 2
@@ -187,15 +195,28 @@
     req_local, heads_dev, head_dim = query.shape
     slot_count, block_len, _, _ = key_cache.shape
     n_inst = lengths.shape[0] // req_local
+    ring_z = n_inst // ring_y
     n_tp = lax.axis_size("tp")
     rows = req_local * heads_dev
     features = out_weight.shape[1]
-    params = pltpu.CompilerParams(vmem_limit_bytes=40 * 1024 * 1024)
+    params = pltpu.CompilerParams(vmem_limit_bytes=24 * 1024 * 1024)
     shape = jax.ShapeDtypeStruct
 
     flat_query = query.reshape(rows, head_dim)
-    copies = jnp.broadcast_to(flat_query[None], (n_inst, rows, head_dim))
-    everyone = lax.all_to_all(copies, "inst", 0, 0, tiled=True)
+    copies = pl.pallas_call(
+        copies_kernel,
+        out_shape=shape((ring_z, rows, head_dim), bf16),
+        in_specs=vmem(1),
+        out_specs=vmem(1)[0],
+        compiler_params=params,
+        cost_estimate=pl.CostEstimate(flops=20_000_000_000, bytes_accessed=1_000_000, transcendentals=0),
+        name="copies",
+    )(flat_query)
+    row = lax.all_to_all(copies, "z", 0, 0, tiled=True).reshape(ring_z * rows, head_dim)
+    from_rows = {0: row}
+    for k in (1, 3, 2):
+        pairs = [(i, (i + k) % ring_y) for i in range(ring_y)]
+        from_rows[k] = lax.ppermute(row, "y", pairs)
     keys = key_cache.reshape(slot_count, block_len, head_dim)
     values = value_cache.reshape(slot_count, block_len, head_dim)
     sent_rows = (lent_slots + 1) * heads_dev
@@ -206,7 +227,7 @@
             shape((slot_count, heads_dev, head_dim), f32),
             shape((slot_count // lent_slots, heads_dev, head_dim), f32),
         ),
-        in_specs=smem(3) + vmem(3),
+        in_specs=smem(3) + vmem(6),
         out_specs=tuple(vmem(3)),
         scratch_shapes=[
             pltpu.VMEM((n_inst * lent_slots + 1, heads_dev, head_dim), f32),
@@ -215,9 +236,9 @@
         ],
         compiler_params=params,
         name="attend",
-    )(block_owner, block_index, lengths, everyone.reshape(n_inst * rows, head_dim), keys, values)
+    )(block_owner, block_index, lengths, *[from_rows[k] for k in range(ring_y)], keys, values)
     got = lax.all_to_all(
-        sent.reshape(n_inst, sent_rows, head_dim), "inst", 0, 0, tiled=True
+        sent.reshape(n_inst, sent_rows, head_dim), inst, 0, 0, tiled=True
     ).reshape(n_inst * sent_rows, head_dim)
     attended, for_core = pl.pallas_call(
         merge_kernel,
@@ -241,9 +262,7 @@
         in_specs=vmem(2),
         out_specs=vmem(1)[0],
         compiler_params=params,
-        cost_estimate=pl.CostEstimate(
-            flops=req_local * heads_dev * head_dim * features, bytes_accessed=4194304, transcendentals=0
-        ),
+        cost_estimate=pl.CostEstimate(flops=200_000_000, bytes_accessed=4_000_000, transcendentals=0),
         name="project",
     )(attended, out_weight)
     width = features // n_tp
@@ -256,24 +275,26 @@
         name="split",
     )(keep, from_core)
     total = own
-    for k in (1, 2, 3):
+    for k in (2, 1, 3):
         pairs = [(i, (i + 2 * k) % n_tp) for i in range(n_tp)]
         total = total + lax.ppermute(parts[k - 1], "tp", pairs).astype(f32)
     return total.astype(bf16)
 
 
 def solution(mesh):
+    shape = (ring_y, mesh.shape["inst"] // ring_y, mesh.shape["tp"])
+    mesh = Mesh(mesh.devices.reshape(shape), ("y", "z", "tp"))
     placed = (
-        P("inst", "tp", None),
-        P("inst", "tp", None),
-        P("inst", "tp", None),
-        P("inst", None, "tp", None),
-        P("inst", None, "tp", None),
+        P(inst, "tp", None),
+        P(inst, "tp", None),
+        P(inst, "tp", None),
+        P(inst, None, "tp", None),
+        P(inst, None, "tp", None),
         P("tp", None),
         P(),
-        P("inst"),
-        P("inst"),
+        P(inst),
+        P(inst),
     )
     return jax.shard_map(
-        body, mesh=mesh, in_specs=placed, out_specs=P("inst", "tp"), check_vma=False
+        body, mesh=mesh, in_specs=placed, out_specs=P(inst, "tp"), check_vma=False
     )

time: 70.4 us -> 58.1 us (0.83)
  blocking collectives: 46.4 us -> 32.9 us
  local copies, waits for them, and re-layouts: 10.9 us -> 0.76 us
  waiting for transfers between devices: 2.22 us -> 8.6 us
  starting transfers between devices: 5.73 us -> 11 us
  Pallas kernels: 4.23 us -> 3.48 us
    all_to_all x2, blocking collectives: 46.4 us -> 32.9 us  [the longest x1 16.8 us: body(): lax.all_to_all(sent.reshape(n_inst, sent_rows, head_dim), inst, 0, 0, til...]
    unnamed x20, local copies, waits for them, and re-layouts: 10 us -> 0.76 us
    ppermute x0 -> x3, waiting for transfers between devices: none -> 6.41 us  [body(): from_rows[k] = lax.ppermute(row, 'y', pairs)]
    ppermute x0 -> x3, starting transfers between devices: none -> 4.61 us  [body(): from_rows[k] = lax.ppermute(row, 'y', pairs)]
    pallas_call x1, Pallas kernels: 1.91 us -> 1.04 us  [body(): pl.pallas_call(merge_kernel, out_shape=(shape((req_local, heads_dev * hea...]
    broadcast_in_dim x1 -> x0, local copies, waits for them, and re-layouts: 0.82 us -> none  [body(): copies = jnp.broadcast_to(flat_query[None], (n_inst, rows, head_dim))]
  transfers between devices with their start and end apart: 4 -> 7, of which waited for: 2 -> 5; matrix products, arithmetic and copies ran while one was open for 0% -> 0% of each run, Pallas kernels for 1% -> 1%
where the time goes in v3:
time: 58.1 us; the launch traced here: 57.4 us
  blocking collectives  32.9 us (57%)
  starting transfers between devices  11 us (19%)
  waiting for transfers between devices  8.6 us (15%)
  Pallas kernels  3.48 us (6%)
  local copies, waits for them, and re-layouts  0.76 us (1%)
  other arithmetic  0.61 us (1%)
    all_to_all x1, blocking collectives, body(): lax.all_to_all(sent.reshape(n_inst, sent_rows, head_dim), inst, 0, 0, til...  16.8 us
    all_to_all x1, blocking collectives, body(): lax.all_to_all(copies, 'z', 0, 0, tiled=True)  16.1 us
    ppermute x3, waiting for transfers between devices, body(): from_rows[k] = lax.ppermute(row, 'y', pairs)  6.41 us
    ppermute x3, starting transfers between devices, body(): total = total + lax.ppermute(parts[k - 1], 'tp', pairs).astype(f32)  6.35 us
    ppermute x3, starting transfers between devices, body(): from_rows[k] = lax.ppermute(row, 'y', pairs)  4.61 us
    pallas_call x1, Pallas kernels, body(): pl.pallas_call(attend_kernel, out_shape=(shape((n_inst * sent_rows, head_...  1.74 us
    ppermute x3, waiting for transfers between devices, body(): total = total + lax.ppermute(parts[k - 1], 'tp', pairs).astype(f32)  1.63 us
  transfers between devices with their start and end apart: 7, of which 5 were waited for; matrix products, arithmetic and copies ran while one was open for 0% of the time, Pallas kernels for 1%

profile of v3, /device:TPU:32, one launch (start us, length us, event | category | flops | bytes accessed | tf_op | source)
XLA Modules:
  0.0 57.4 jit_solution(17885877229388503993)
XLA Ops:
  0.0 0.7 %copy-done.3 = bf16[8,8,128]{2,1,0:T(8,128)(2,1)S(1)} copy-done((bf16[8,8,128]{2,1,0:T(8,128)(2,1)S(1)}, bf16[8,8,128]{2,1,0:T(8,128)(2,1)}, u32[]{:S(2)}) %copy-start.3) | copy-done | bytes 16408
  0.7 0.0 copy-start.9
  0.7 0.0 copy-start
  0.8 16.1 %all_to_all.10 = bf16[8,64,128]{2,1,0:T(8,128)(2,1)S(1)} all-to-all(bf16[8,64,128]{2,1,0:T(8,128)(2,1)S(1)} %copies.1), channel_id=1, replica_groups=mesh['y'=4,'z'=8,'tp'=8] {'z'}, dimensions={0} | all-to-all | bytes 262144 | tf_op jit(solution)/shard_map/all_to_all | solution.py:215
  16.9 3.0 %collective-permute-start.2 = (bf16[512,128]{1,0:T(8,128)(2,1)S(1)}, bf16[512,128]{1,0:T(8,128)(2,1)S(1)}, u32[]{:S(2)}, u32[]{:S(2)}) collective-permute-start(bf16[512,128]{1,0:T(8,128)(2,1)S(1)} %bitcast.11), channel_id=1, source_target_pairs={{0,192},{64,0},{128,64},{192,128},{1,193},{65,1},{129,65},{193,129... | collective-permute-start | bytes 393224 | tf_op jit(solution)/shard_map/ppermute | solution.py:219
  19.9 0.6 %collective-permute-start.1 = (bf16[512,128]{1,0:T(8,128)(2,1)S(1)}, bf16[512,128]{1,0:T(8,128)(2,1)S(1)}, u32[]{:S(2)}, u32[]{:S(2)}) collective-permute-start(bf16[512,128]{1,0:T(8,128)(2,1)S(1)} %bitcast.12), channel_id=1, source_target_pairs={{0,128},{64,192},{128,0},{192,64},{1,129},{65,193},{129,1},{193,65... | collective-permute-start | bytes 393224 | tf_op jit(solution)/shard_map/ppermute | solution.py:219
  20.5 1.0 %collective-permute-start = (bf16[512,128]{1,0:T(8,128)(2,1)S(1)}, bf16[512,128]{1,0:T(8,128)(2,1)S(1)}, u32[]{:S(2)}, u32[]{:S(2)}) collective-permute-start(bf16[512,128]{1,0:T(8,128)(2,1)S(1)} %bitcast.13), channel_id=1, source_target_pairs={{0,64},{64,128},{128,192},{192,0},{1,65},{65,129},{129,193},{193,1... | collective-permute-start | bytes 393224 | tf_op jit(solution)/shard_map/ppermute | solution.py:219
  21.5 2.9 %collective-permute-done.2.row3_ref = bf16[512,128]{1,0:T(8,128)(2,1)S(1)} collective-permute-done((bf16[512,128]{1,0:T(8,128)(2,1)S(1)}, bf16[512,128]{1,0:T(8,128)(2,1)S(1)}, u32[]{:S(2)}, u32[]{:S(2)}) %collective-permute-start.2) | collective-permute-done | bytes 131104 | tf_op jit(solution)/shard_map/ppermute | solution.py:219
  24.3 2.2 %collective-permute-done.1.row2_ref = bf16[512,128]{1,0:T(8,128)(2,1)S(1)} collective-permute-done((bf16[512,128]{1,0:T(8,128)(2,1)S(1)}, bf16[512,128]{1,0:T(8,128)(2,1)S(1)}, u32[]{:S(2)}, u32[]{:S(2)}) %collective-permute-start.1) | collective-permute-done | bytes 131104 | tf_op jit(solution)/shard_map/ppermute | solution.py:219
  26.6 1.3 %collective-permute-done.row1_ref = bf16[512,128]{1,0:T(8,128)(2,1)S(1)} collective-permute-done((bf16[512,128]{1,0:T(8,128)(2,1)S(1)}, bf16[512,128]{1,0:T(8,128)(2,1)S(1)}, u32[]{:S(2)}, u32[]{:S(2)}) %collective-permute-start) | collective-permute-done | bytes 131104 | tf_op jit(solution)/shard_map/ppermute | solution.py:219
  27.9 0.0 copy-done.1
  27.9 0.0 copy-done.2
  27.9 0.0 copy-done.7
  27.9 0.0 copy-done.8
  27.9 0.0 copy-done.9
  27.9 0.0 copy-start.4
  27.9 0.0 copy-start.5
  27.9 0.0 copy-start.6
  28.0 1.7 %attend.1 = (bf16[1280,128]{1,0:T(8,128)(2,1)S(1)}, f32[32,8,128]{2,1,0:T(8,128)S(1)}, f32[8,8,128]{2,1,0:T(8,128)S(1)}) custom-call(s32[32]{0:T(128)S(1)} %copy-done.8, s32[32]{0:T(128)S(1)} %copy-done.9, s32[256]{0:T(256)S(1)} %copy-done.7, bf16[512,128]{1,0:T(8,128)(2,1)S(1)} %bitcast.14, bf16[512,128]{1,0:T(8,128)(2,1)S(1)} %collective-permute-done.row1_ref, ...), custom_call_target="tpu_custom_call" | custom-call | tf_op jit(solution)/shard_map/attend/pallas_call | solution.py:223
  29.7 16.8 %all_to_all.11 = bf16[32,40,128]{2,1,0:T(8,128)(2,1)S(1)} all-to-all(bf16[32,40,128]{2,1,0:T(8,128)(2,1)S(1)} %bitcast.15), channel_id=1, replica_groups=mesh['y'=4,'z'=8,'tp'=8] {'y','z'}, dimensions={0} | all-to-all | bytes 655360 | tf_op jit(solution)/shard_map/all_to_all | solution.py:240
  46.6 0.0 copy-done.6
  46.6 1.0 %merge.1 = (bf16[8,1024]{1,0:T(8,128)(2,1)S(1)}, bf16[8,2048]{1,0:T(8,128)(2,1)S(1)}) custom-call(bf16[1280,128]{1,0:T(8,128)(2,1)S(1)} %bitcast.10, f32[32,8,128]{2,1,0:T(8,128)S(1)} %get-tuple-element.15.local_out_ref, f32[8,8,128]{2,1,0:T(8,128)S(1)} %get-tuple-element.16.local_note_ref, bf16[64,128]{1,0:T(8,128)(2,1)S(1)} %bitcast.17, ...), custom_call_target="tpu_custom_call" | custom-call | tf_op jit(solution)/shard_map/merge/pallas_call | solution.py:243
  47.6 0.0 collective-permute-start.3
  47.6 0.7 %project.1.keep_ref = f32[8,2048]{1,0:T(8,128)S(1)} custom-call(bf16[8,1024]{1,0:T(8,128)(2,1)S(1)} %get-tuple-element.17.attended_ref, bf16[1024,4096]{1,0:T(8,128)(2,1)S(1)} %copy-done), custom_call_target="tpu_custom_call" | custom-call | flops 200000000 | bytes 4000000 | tf_op jit(solution)/shard_map/project/pallas_call | solution.py:259
  48.3 0.6 collective-permute-done.3.got_ref
  48.9 3.1 %collective-permute-start.4 = (bf16[8,512]{1,0:T(8,128)(2,1)S(1)}, bf16[8,512]{1,0:T(8,128)(2,1)S(1)}, u32[]{:S(2)}, u32[]{:S(2)}) collective-permute-start(bf16[8,512]{1,0:T(8,128)(2,1)S(1)} %get-tuple-element.20), channel_id=1, source_target_pairs={{0,4},{1,5},{2,6},{3,7},{4,0},{5,1},{6,2},{7,3},{8,12},{9,13},{10,... | collective-permute-start | bytes 24584 | tf_op jit(solution)/shard_map/ppermute | solution.py:280
  52.0 0.6 %collective-permute-start.5 = (bf16[8,512]{1,0:T(8,128)(2,1)S(1)}, bf16[8,512]{1,0:T(8,128)(2,1)S(1)}, u32[]{:S(2)}, u32[]{:S(2)}) collective-permute-start(bf16[8,512]{1,0:T(8,128)(2,1)S(1)} %get-tuple-element.21), channel_id=1, source_target_pairs={{0,2},{1,3},{2,4},{3,5},{4,6},{5,7},{6,0},{7,1},{8,10},{9,11},{10,... | collective-permute-start | bytes 24584 | tf_op jit(solution)/shard_map/ppermute | solution.py:280
  52.6 2.6 %collective-permute-start.6 = (bf16[8,512]{1,0:T(8,128)(2,1)S(1)}, bf16[8,512]{1,0:T(8,128)(2,1)S(1)}, u32[]{:S(2)}, u32[]{:S(2)}) collective-permute-start(bf16[8,512]{1,0:T(8,128)(2,1)S(1)} %get-tuple-element.22), channel_id=1, source_target_pairs={{0,6},{1,7},{2,0},{3,1},{4,2},{5,3},{6,4},{7,5},{8,14},{9,15},{10,... | collective-permute-start | bytes 24584 | tf_op jit(solution)/shard_map/ppermute | solution.py:280
  55.2 0.0 collective-permute-done.4
  55.2 1.6 %collective-permute-done.5 = bf16[8,512]{1,0:T(8,128)(2,1)S(1)} collective-permute-done((bf16[8,512]{1,0:T(8,128)(2,1)S(1)}, bf16[8,512]{1,0:T(8,128)(2,1)S(1)}, u32[]{:S(2)}, u32[]{:S(2)}) %collective-permute-start.5) | collective-permute-done | bytes 8224 | tf_op jit(solution)/shard_map/ppermute | solution.py:280
  56.8 0.0 collective-permute-done.6
  56.8 0.6 %add_convert_fusion = bf16[8,512]{1,0:T(8,128)(2,1)} fusion(bf16[8,512]{1,0:T(8,128)(2,1)S(1)} %collective-permute-done.6, bf16[8,512]{1,0:T(8,128)(2,1)S(1)} %collective-permute-done.5, f32[8,512]{1,0:T(8,128)S(1)} %get-tuple-element.19, bf16[8,512]{1,0:T(8,128)(2,1)S(1)} %collective-permute-done.4), kind=kLoop, calls=%fused_computation | loop fusion | flops 28672 | bytes 49152 | tf_op jit(solution)/shard_map/convert_element_type | solution.py:281
  (10 shorter events, 0.0 us)
Async XLA Ops:
  0.0 0.7 %copy-start.3 = (bf16[8,8,128]{2,1,0:T(8,128)(2,1)S(1)}, bf16[8,8,128]{2,1,0:T(8,128)(2,1)}, u32[]{:S(2)}) copy-start(bf16[8,8,128]{2,1,0:T(8,128)(2,1)} %param.9) | copy-start | bytes 49156
  0.7 27.2 %copy-start.1 = (bf16[32,256,1,128]{3,1,2,0:T(8,128)(2,1)S(1)}, bf16[32,256,1,128]{3,1,2,0:T(8,128)(2,1)}, u32[]{:S(2)}) copy-start(bf16[32,256,1,128]{3,1,2,0:T(8,128)(2,1)} %param.12) | copy-start | bytes 6291460
  0.7 27.2 %copy-start.2 = (bf16[32,256,1,128]{3,1,2,0:T(8,128)(2,1)S(1)}, bf16[32,256,1,128]{3,1,2,0:T(8,128)(2,1)}, u32[]{:S(2)}) copy-start(bf16[32,256,1,128]{3,1,2,0:T(8,128)(2,1)} %param.13) | copy-start | bytes 6291460
  0.7 27.2 %copy-start.7 = (s32[256]{0:T(256)S(1)}, s32[256]{0:T(256)}, u32[]{:S(2)}) copy-start(s32[256]{0:T(256)} %length_ref.1) | copy-start | bytes 3076
  0.7 27.2 %copy-start.8 = (s32[32]{0:T(128)S(1)}, s32[32]{0:T(128)}, u32[]{:S(2)}) copy-start(s32[32]{0:T(128)} %owner_ref.1) | copy-start | bytes 388
  0.7 27.2 %copy-start.9 = (s32[32]{0:T(128)S(1)}, s32[32]{0:T(128)}, u32[]{:S(2)}) copy-start(s32[32]{0:T(128)} %index_ref.1) | copy-start | bytes 388
  0.7 45.8 %copy-start = (bf16[1024,4096]{1,0:T(8,128)(2,1)S(1)}, bf16[1024,4096]{1,0:T(8,128)(2,1)}, u32[]{:S(2)}) copy-start(bf16[1024,4096]{1,0:T(8,128)(2,1)} %weight_ref.3) | copy-start | bytes 25165828
  16.9 7.5 %collective-permute-start.2 = (bf16[512,128]{1,0:T(8,128)(2,1)S(1)}, bf16[512,128]{1,0:T(8,128)(2,1)S(1)}, u32[]{:S(2)}, u32[]{:S(2)}) collective-permute-start(bf16[512,128]{1,0:T(8,128)(2,1)S(1)} %bitcast.11), channel_id=1, source_target_pairs={{0,192},{64,0},{128,64},{192,128},{1,193},{65,1},{129,65},{193,129... | collective-permute-start | bytes 393224 | tf_op jit(solution)/shard_map/ppermute | solution.py:219
  19.9 6.7 %collective-permute-start.1 = (bf16[512,128]{1,0:T(8,128)(2,1)S(1)}, bf16[512,128]{1,0:T(8,128)(2,1)S(1)}, u32[]{:S(2)}, u32[]{:S(2)}) collective-permute-start(bf16[512,128]{1,0:T(8,128)(2,1)S(1)} %bitcast.12), channel_id=1, source_target_pairs={{0,128},{64,192},{128,0},{192,64},{1,129},{65,193},{129,1},{193,65... | collective-permute-start | bytes 393224 | tf_op jit(solution)/shard_map/ppermute | solution.py:219
  20.5 7.4 %collective-permute-start = (bf16[512,128]{1,0:T(8,128)(2,1)S(1)}, bf16[512,128]{1,0:T(8,128)(2,1)S(1)}, u32[]{:S(2)}, u32[]{:S(2)}) collective-permute-start(bf16[512,128]{1,0:T(8,128)(2,1)S(1)} %bitcast.13), channel_id=1, source_target_pairs={{0,64},{64,128},{128,192},{192,0},{1,65},{65,129},{129,193},{193,1... | collective-permute-start | bytes 393224 | tf_op jit(solution)/shard_map/ppermute | solution.py:219
  27.9 18.6 %copy-start.4 = (bf16[8,8,128]{2,1,0:T(8,128)(2,1)S(1)}, bf16[8,8,128]{2,1,0:T(8,128)(2,1)}, u32[]{:S(2)}) copy-start(bf16[8,8,128]{2,1,0:T(8,128)(2,1)} %param.9) | copy-start | bytes 49156
  27.9 18.6 %copy-start.5 = (bf16[8,1,128]{2,0,1:T(8,128)(2,1)S(1)}, bf16[8,1,128]{2,0,1:T(8,128)(2,1)}, u32[]{:S(2)}) copy-start(bf16[8,1,128]{2,0,1:T(8,128)(2,1)} %param.10) | copy-start | bytes 6148
  27.9 18.6 %copy-start.6 = (bf16[8,1,128]{2,0,1:T(8,128)(2,1)S(1)}, bf16[8,1,128]{2,0,1:T(8,128)(2,1)}, u32[]{:S(2)}) copy-start(bf16[8,1,128]{2,0,1:T(8,128)(2,1)} %param.11) | copy-start | bytes 6148
  47.6 1.2 %collective-permute-start.3 = (bf16[8,2048]{1,0:T(8,128)(2,1)S(1)}, bf16[8,2048]{1,0:T(8,128)(2,1)S(1)}, u32[]{:S(2)}, u32[]{:S(2)}) collective-permute-start(bf16[8,2048]{1,0:T(8,128)(2,1)S(1)} %get-tuple-element.18), channel_id=1, source_target_pairs={{0,1},{1,0},{2,3},{3,2},{4,5},{5,4},{6,7},{7,6},{8,9},{9,8},{10,11... | collective-permute-start | bytes 98312 | tf_op jit(solution)/shard_map/ppermute | solution.py:258
  48.9 6.3 %collective-permute-start.4 = (bf16[8,512]{1,0:T(8,128)(2,1)S(1)}, bf16[8,512]{1,0:T(8,128)(2,1)S(1)}, u32[]{:S(2)}, u32[]{:S(2)}) collective-permute-start(bf16[8,512]{1,0:T(8,128)(2,1)S(1)} %get-tuple-element.20), channel_id=1, source_target_pairs={{0,4},{1,5},{2,6},{3,7},{4,0},{5,1},{6,2},{7,3},{8,12},{9,13},{10,... | collective-permute-start | bytes 24584 | tf_op jit(solution)/shard_map/ppermute | solution.py:280
  52.0 4.9 %collective-permute-start.5 = (bf16[8,512]{1,0:T(8,128)(2,1)S(1)}, bf16[8,512]{1,0:T(8,128)(2,1)S(1)}, u32[]{:S(2)}, u32[]{:S(2)}) collective-permute-start(bf16[8,512]{1,0:T(8,128)(2,1)S(1)} %get-tuple-element.21), channel_id=1, source_target_pairs={{0,2},{1,3},{2,4},{3,5},{4,6},{5,7},{6,0},{7,1},{8,10},{9,11},{10,... | collective-permute-start | bytes 24584 | tf_op jit(solution)/shard_map/ppermute | solution.py:280
  52.6 4.3 %collective-permute-start.6 = (bf16[8,512]{1,0:T(8,128)(2,1)S(1)}, bf16[8,512]{1,0:T(8,128)(2,1)S(1)}, u32[]{:S(2)}, u32[]{:S(2)}) collective-permute-start(bf16[8,512]{1,0:T(8,128)(2,1)S(1)} %get-tuple-element.22), channel_id=1, source_target_pairs={{0,6},{1,7},{2,0},{3,1},{4,2},{5,3},{6,4},{7,5},{8,14},{9,15},{10,... | collective-permute-start | bytes 24584 | tf_op jit(solution)/shard_map/ppermute | solution.py:280

commit v4 on v3

--- a/solution.py
+++ b/solution.py
@@ -20,7 +20,7 @@
 
 
 def attend_kernel(
-    owner_ref, index_ref, length_ref, row0_ref, row1_ref, row2_ref, row3_ref, key_ref, value_ref,
+    owner_ref, index_ref, length_ref, row0_ref, row2_ref, row3_ref, row1_ref, key_ref, value_ref,
     sent_ref, local_out_ref, local_note_ref, entry_out, entry_note, used_count,
 ):
     slots, block_len, head_dim = key_ref.shape
@@ -236,7 +236,7 @@
         ],
         compiler_params=params,
         name="attend",
-    )(block_owner, block_index, lengths, *[from_rows[k] for k in range(ring_y)], keys, values)
+    )(block_owner, block_index, lengths, *[from_rows[k] for k in (0, 2, 3, 1)], keys, values)
     got = lax.all_to_all(
         sent.reshape(n_inst, sent_rows, head_dim), inst, 0, 0, tiled=True
     ).reshape(n_inst * sent_rows, head_dim)

time: 58.1 us -> 57.2 us (0.985)
  waiting for transfers between devices: 8.6 us -> 6.67 us
  starting transfers between devices: 11 us -> 11.6 us
    ppermute x3, waiting for transfers between devices: 6.41 us -> 4.49 us  [body(): from_rows[k] = lax.ppermute(row, 'y', pairs)]
    ppermute x3, starting transfers between devices: 4.61 us -> 5.22 us  [body(): from_rows[k] = lax.ppermute(row, 'y', pairs)]
  transfers between devices with their start and end apart: 7 -> 7, of which waited for: 5 -> 4; matrix products, arithmetic and copies ran while one was open for 0% -> 0% of each run, Pallas kernels for 1% -> 1%
where the time goes in v4:
time: 57.2 us; the launch traced here: 56.5 us
  blocking collectives  33.3 us (58%)
  starting transfers between devices  11.6 us (20%)
  waiting for transfers between devices  6.67 us (12%)
  Pallas kernels  3.48 us (6%)
  local copies, waits for them, and re-layouts  0.76 us (1%)
  other arithmetic  0.61 us (1%)
    all_to_all x1, blocking collectives, body(): lax.all_to_all(sent.reshape(n_inst, sent_rows, head_dim), inst, 0, 0, til...  17.2 us
    all_to_all x1, blocking collectives, body(): lax.all_to_all(copies, 'z', 0, 0, tiled=True)  16.1 us
    ppermute x3, starting transfers between devices, body(): total = total + lax.ppermute(parts[k - 1], 'tp', pairs).astype(f32)  6.35 us
    ppermute x3, starting transfers between devices, body(): from_rows[k] = lax.ppermute(row, 'y', pairs)  5.22 us
    ppermute x3, waiting for transfers between devices, body(): from_rows[k] = lax.ppermute(row, 'y', pairs)  4.49 us
    pallas_call x1, Pallas kernels, body(): pl.pallas_call(attend_kernel, out_shape=(shape((n_inst * sent_rows, head_...  1.74 us
    ppermute x3, waiting for transfers between devices, body(): total = total + lax.ppermute(parts[k - 1], 'tp', pairs).astype(f32)  1.63 us
  transfers between devices with their start and end apart: 7, of which 4 were waited for; matrix products, arithmetic and copies ran while one was open for 0% of the time, Pallas kernels for 1%

profile of v4, /device:TPU:32, one launch (start us, length us, event | category | flops | bytes accessed | tf_op | source)
XLA Modules:
  0.0 56.5 jit_solution(2531076796866294111)
XLA Ops:
  0.0 0.7 %copy-done.3 = bf16[8,8,128]{2,1,0:T(8,128)(2,1)S(1)} copy-done((bf16[8,8,128]{2,1,0:T(8,128)(2,1)S(1)}, bf16[8,8,128]{2,1,0:T(8,128)(2,1)}, u32[]{:S(2)}) %copy-start.3) | copy-done | bytes 16408
  0.7 0.0 copy-start.9
  0.7 0.0 copy-start
  0.8 16.1 %all_to_all.10 = bf16[8,64,128]{2,1,0:T(8,128)(2,1)S(1)} all-to-all(bf16[8,64,128]{2,1,0:T(8,128)(2,1)S(1)} %copies.1), channel_id=1, replica_groups=mesh['y'=4,'z'=8,'tp'=8] {'z'}, dimensions={0} | all-to-all | bytes 262144 | tf_op jit(solution)/shard_map/all_to_all | solution.py:215
  16.9 1.6 %collective-permute-start.2 = (bf16[512,128]{1,0:T(8,128)(2,1)S(1)}, bf16[512,128]{1,0:T(8,128)(2,1)S(1)}, u32[]{:S(2)}, u32[]{:S(2)}) collective-permute-start(bf16[512,128]{1,0:T(8,128)(2,1)S(1)} %bitcast.11), channel_id=1, source_target_pairs={{0,64},{64,128},{128,192},{192,0},{1,65},{65,129},{129,193},{193,1... | collective-permute-start | bytes 393224 | tf_op jit(solution)/shard_map/ppermute | solution.py:219
  18.4 1.7 %collective-permute-start.1 = (bf16[512,128]{1,0:T(8,128)(2,1)S(1)}, bf16[512,128]{1,0:T(8,128)(2,1)S(1)}, u32[]{:S(2)}, u32[]{:S(2)}) collective-permute-start(bf16[512,128]{1,0:T(8,128)(2,1)S(1)} %bitcast.12), channel_id=1, source_target_pairs={{0,192},{64,0},{128,64},{192,128},{1,193},{65,1},{129,65},{193,129... | collective-permute-start | bytes 393224 | tf_op jit(solution)/shard_map/ppermute | solution.py:219
  20.1 2.0 %collective-permute-start = (bf16[512,128]{1,0:T(8,128)(2,1)S(1)}, bf16[512,128]{1,0:T(8,128)(2,1)S(1)}, u32[]{:S(2)}, u32[]{:S(2)}) collective-permute-start(bf16[512,128]{1,0:T(8,128)(2,1)S(1)} %bitcast.13), channel_id=1, source_target_pairs={{0,128},{64,192},{128,0},{192,64},{1,129},{65,193},{129,1},{193,65... | collective-permute-start | bytes 393224 | tf_op jit(solution)/shard_map/ppermute | solution.py:219
  22.1 2.2 %collective-permute-done.2.row1_ref = bf16[512,128]{1,0:T(8,128)(2,1)S(1)} collective-permute-done((bf16[512,128]{1,0:T(8,128)(2,1)S(1)}, bf16[512,128]{1,0:T(8,128)(2,1)S(1)}, u32[]{:S(2)}, u32[]{:S(2)}) %collective-permute-start.2) | collective-permute-done | bytes 131104 | tf_op jit(solution)/shard_map/ppermute | solution.py:219
  24.3 0.0 collective-permute-done.1.row3_ref
  24.3 2.2 %collective-permute-done.row2_ref = bf16[512,128]{1,0:T(8,128)(2,1)S(1)} collective-permute-done((bf16[512,128]{1,0:T(8,128)(2,1)S(1)}, bf16[512,128]{1,0:T(8,128)(2,1)S(1)}, u32[]{:S(2)}, u32[]{:S(2)}) %collective-permute-start) | collective-permute-done | bytes 131104 | tf_op jit(solution)/shard_map/ppermute | solution.py:219
  26.6 0.0 copy-done.1
  26.6 0.0 copy-done.2
  26.6 0.0 copy-done.7
  26.6 0.0 copy-done.8
  26.6 0.0 copy-done.9
  26.6 0.0 copy-start.4
  26.6 0.0 copy-start.5
  26.6 0.0 copy-start.6
  26.6 1.7 %attend.1 = (bf16[1280,128]{1,0:T(8,128)(2,1)S(1)}, f32[32,8,128]{2,1,0:T(8,128)S(1)}, f32[8,8,128]{2,1,0:T(8,128)S(1)}) custom-call(s32[32]{0:T(128)S(1)} %copy-done.8, s32[32]{0:T(128)S(1)} %copy-done.9, s32[256]{0:T(256)S(1)} %copy-done.7, bf16[512,128]{1,0:T(8,128)(2,1)S(1)} %bitcast.14, bf16[512,128]{1,0:T(8,128)(2,1)S(1)} %collective-permute-done.row2_ref, ...), custom_call_target="tpu_custom_call" | custom-call | tf_op jit(solution)/shard_map/attend/pallas_call | solution.py:223
  28.4 17.2 %all_to_all.11 = bf16[32,40,128]{2,1,0:T(8,128)(2,1)S(1)} all-to-all(bf16[32,40,128]{2,1,0:T(8,128)(2,1)S(1)} %bitcast.15), channel_id=1, replica_groups=mesh['y'=4,'z'=8,'tp'=8] {'y','z'}, dimensions={0} | all-to-all | bytes 655360 | tf_op jit(solution)/shard_map/all_to_all | solution.py:240
  45.6 0.0 copy-done.4
  45.6 1.0 %merge.1 = (bf16[8,1024]{1,0:T(8,128)(2,1)S(1)}, bf16[8,2048]{1,0:T(8,128)(2,1)S(1)}) custom-call(bf16[1280,128]{1,0:T(8,128)(2,1)S(1)} %bitcast.10, f32[32,8,128]{2,1,0:T(8,128)S(1)} %get-tuple-element.15.local_out_ref, f32[8,8,128]{2,1,0:T(8,128)S(1)} %get-tuple-element.16.local_note_ref, bf16[64,128]{1,0:T(8,128)(2,1)S(1)} %bitcast.17, ...), custom_call_target="tpu_custom_call" | custom-call | tf_op jit(solution)/shard_map/merge/pallas_call | solution.py:243
  46.7 0.0 collective-permute-start.3
  46.7 0.7 %project.1.keep_ref = f32[8,2048]{1,0:T(8,128)S(1)} custom-call(bf16[8,1024]{1,0:T(8,128)(2,1)S(1)} %get-tuple-element.17.attended_ref, bf16[1024,4096]{1,0:T(8,128)(2,1)S(1)} %copy-done), custom_call_target="tpu_custom_call" | custom-call | flops 200000000 | bytes 4000000 | tf_op jit(solution)/shard_map/project/pallas_call | solution.py:259
  47.3 0.6 collective-permute-done.3.got_ref
  47.9 3.1 %collective-permute-start.4 = (bf16[8,512]{1,0:T(8,128)(2,1)S(1)}, bf16[8,512]{1,0:T(8,128)(2,1)S(1)}, u32[]{:S(2)}, u32[]{:S(2)}) collective-permute-start(bf16[8,512]{1,0:T(8,128)(2,1)S(1)} %get-tuple-element.20), channel_id=1, source_target_pairs={{0,4},{1,5},{2,6},{3,7},{4,0},{5,1},{6,2},{7,3},{8,12},{9,13},{10,... | collective-permute-start | bytes 24584 | tf_op jit(solution)/shard_map/ppermute | solution.py:280
  51.0 0.6 %collective-permute-start.5 = (bf16[8,512]{1,0:T(8,128)(2,1)S(1)}, bf16[8,512]{1,0:T(8,128)(2,1)S(1)}, u32[]{:S(2)}, u32[]{:S(2)}) collective-permute-start(bf16[8,512]{1,0:T(8,128)(2,1)S(1)} %get-tuple-element.21), channel_id=1, source_target_pairs={{0,2},{1,3},{2,4},{3,5},{4,6},{5,7},{6,0},{7,1},{8,10},{9,11},{10,... | collective-permute-start | bytes 24584 | tf_op jit(solution)/shard_map/ppermute | solution.py:280
  51.6 2.6 %collective-permute-start.6 = (bf16[8,512]{1,0:T(8,128)(2,1)S(1)}, bf16[8,512]{1,0:T(8,128)(2,1)S(1)}, u32[]{:S(2)}, u32[]{:S(2)}) collective-permute-start(bf16[8,512]{1,0:T(8,128)(2,1)S(1)} %get-tuple-element.22), channel_id=1, source_target_pairs={{0,6},{1,7},{2,0},{3,1},{4,2},{5,3},{6,4},{7,5},{8,14},{9,15},{10,... | collective-permute-start | bytes 24584 | tf_op jit(solution)/shard_map/ppermute | solution.py:280
  54.3 0.0 collective-permute-done.4
  54.3 1.6 %collective-permute-done.5 = bf16[8,512]{1,0:T(8,128)(2,1)S(1)} collective-permute-done((bf16[8,512]{1,0:T(8,128)(2,1)S(1)}, bf16[8,512]{1,0:T(8,128)(2,1)S(1)}, u32[]{:S(2)}, u32[]{:S(2)}) %collective-permute-start.5) | collective-permute-done | bytes 8224 | tf_op jit(solution)/shard_map/ppermute | solution.py:280
  55.9 0.0 collective-permute-done.6
  55.9 0.6 %add_convert_fusion = bf16[8,512]{1,0:T(8,128)(2,1)} fusion(bf16[8,512]{1,0:T(8,128)(2,1)S(1)} %collective-permute-done.6, bf16[8,512]{1,0:T(8,128)(2,1)S(1)} %collective-permute-done.5, f32[8,512]{1,0:T(8,128)S(1)} %get-tuple-element.19, bf16[8,512]{1,0:T(8,128)(2,1)S(1)} %collective-permute-done.4), kind=kLoop, calls=%fused_computation | loop fusion | flops 28672 | bytes 49152 | tf_op jit(solution)/shard_map/convert_element_type | solution.py:281
  (10 shorter events, 0.1 us)
Async XLA Ops:
  0.0 0.7 %copy-start.3 = (bf16[8,8,128]{2,1,0:T(8,128)(2,1)S(1)}, bf16[8,8,128]{2,1,0:T(8,128)(2,1)}, u32[]{:S(2)}) copy-start(bf16[8,8,128]{2,1,0:T(8,128)(2,1)} %param.9) | copy-start | bytes 49156
  0.7 25.8 %copy-start.1 = (bf16[32,256,1,128]{3,1,2,0:T(8,128)(2,1)S(1)}, bf16[32,256,1,128]{3,1,2,0:T(8,128)(2,1)}, u32[]{:S(2)}) copy-start(bf16[32,256,1,128]{3,1,2,0:T(8,128)(2,1)} %param.12) | copy-start | bytes 6291460
  0.7 25.8 %copy-start.2 = (bf16[32,256,1,128]{3,1,2,0:T(8,128)(2,1)S(1)}, bf16[32,256,1,128]{3,1,2,0:T(8,128)(2,1)}, u32[]{:S(2)}) copy-start(bf16[32,256,1,128]{3,1,2,0:T(8,128)(2,1)} %param.13) | copy-start | bytes 6291460
  0.7 25.8 %copy-start.7 = (s32[256]{0:T(256)S(1)}, s32[256]{0:T(256)}, u32[]{:S(2)}) copy-start(s32[256]{0:T(256)} %length_ref.1) | copy-start | bytes 3076
  0.7 25.9 %copy-start.8 = (s32[32]{0:T(128)S(1)}, s32[32]{0:T(128)}, u32[]{:S(2)}) copy-start(s32[32]{0:T(128)} %owner_ref.1) | copy-start | bytes 388
  0.7 25.9 %copy-start.9 = (s32[32]{0:T(128)S(1)}, s32[32]{0:T(128)}, u32[]{:S(2)}) copy-start(s32[32]{0:T(128)} %index_ref.1) | copy-start | bytes 388
  0.7 44.9 %copy-start = (bf16[1024,4096]{1,0:T(8,128)(2,1)S(1)}, bf16[1024,4096]{1,0:T(8,128)(2,1)}, u32[]{:S(2)}) copy-start(bf16[1024,4096]{1,0:T(8,128)(2,1)} %weight_ref.3) | copy-start | bytes 25165828
  16.9 7.5 %collective-permute-start.2 = (bf16[512,128]{1,0:T(8,128)(2,1)S(1)}, bf16[512,128]{1,0:T(8,128)(2,1)S(1)}, u32[]{:S(2)}, u32[]{:S(2)}) collective-permute-start(bf16[512,128]{1,0:T(8,128)(2,1)S(1)} %bitcast.11), channel_id=1, source_target_pairs={{0,64},{64,128},{128,192},{192,0},{1,65},{65,129},{129,193},{193,1... | collective-permute-start | bytes 393224 | tf_op jit(solution)/shard_map/ppermute | solution.py:219
  18.4 5.9 %collective-permute-start.1 = (bf16[512,128]{1,0:T(8,128)(2,1)S(1)}, bf16[512,128]{1,0:T(8,128)(2,1)S(1)}, u32[]{:S(2)}, u32[]{:S(2)}) collective-permute-start(bf16[512,128]{1,0:T(8,128)(2,1)S(1)} %bitcast.12), channel_id=1, source_target_pairs={{0,192},{64,0},{128,64},{192,128},{1,193},{65,1},{129,65},{193,129... | collective-permute-start | bytes 393224 | tf_op jit(solution)/shard_map/ppermute | solution.py:219
  20.1 6.5 %collective-permute-start = (bf16[512,128]{1,0:T(8,128)(2,1)S(1)}, bf16[512,128]{1,0:T(8,128)(2,1)S(1)}, u32[]{:S(2)}, u32[]{:S(2)}) collective-permute-start(bf16[512,128]{1,0:T(8,128)(2,1)S(1)} %bitcast.13), channel_id=1, source_target_pairs={{0,128},{64,192},{128,0},{192,64},{1,129},{65,193},{129,1},{193,65... | collective-permute-start | bytes 393224 | tf_op jit(solution)/shard_map/ppermute | solution.py:219
  26.6 19.0 %copy-start.4 = (bf16[8,8,128]{2,1,0:T(8,128)(2,1)S(1)}, bf16[8,8,128]{2,1,0:T(8,128)(2,1)}, u32[]{:S(2)}) copy-start(bf16[8,8,128]{2,1,0:T(8,128)(2,1)} %param.9) | copy-start | bytes 49156
  26.6 19.0 %copy-start.5 = (bf16[8,1,128]{2,0,1:T(8,128)(2,1)S(1)}, bf16[8,1,128]{2,0,1:T(8,128)(2,1)}, u32[]{:S(2)}) copy-start(bf16[8,1,128]{2,0,1:T(8,128)(2,1)} %param.10) | copy-start | bytes 6148
  26.6 19.0 %copy-start.6 = (bf16[8,1,128]{2,0,1:T(8,128)(2,1)S(1)}, bf16[8,1,128]{2,0,1:T(8,128)(2,1)}, u32[]{:S(2)}) copy-start(bf16[8,1,128]{2,0,1:T(8,128)(2,1)} %param.11) | copy-start | bytes 6148
  46.7 1.2 %collective-permute-start.3 = (bf16[8,2048]{1,0:T(8,128)(2,1)S(1)}, bf16[8,2048]{1,0:T(8,128)(2,1)S(1)}, u32[]{:S(2)}, u32[]{:S(2)}) collective-permute-start(bf16[8,2048]{1,0:T(8,128)(2,1)S(1)} %get-tuple-element.18), channel_id=1, source_target_pairs={{0,1},{1,0},{2,3},{3,2},{4,5},{5,4},{6,7},{7,6},{8,9},{9,8},{10,11... | collective-permute-start | bytes 98312 | tf_op jit(solution)/shard_map/ppermute | solution.py:258
  47.9 6.4 %collective-permute-start.4 = (bf16[8,512]{1,0:T(8,128)(2,1)S(1)}, bf16[8,512]{1,0:T(8,128)(2,1)S(1)}, u32[]{:S(2)}, u32[]{:S(2)}) collective-permute-start(bf16[8,512]{1,0:T(8,128)(2,1)S(1)} %get-tuple-element.20), channel_id=1, source_target_pairs={{0,4},{1,5},{2,6},{3,7},{4,0},{5,1},{6,2},{7,3},{8,12},{9,13},{10,... | collective-permute-start | bytes 24584 | tf_op jit(solution)/shard_map/ppermute | solution.py:280
  51.0 4.9 %collective-permute-start.5 = (bf16[8,512]{1,0:T(8,128)(2,1)S(1)}, bf16[8,512]{1,0:T(8,128)(2,1)S(1)}, u32[]{:S(2)}, u32[]{:S(2)}) collective-permute-start(bf16[8,512]{1,0:T(8,128)(2,1)S(1)} %get-tuple-element.21), channel_id=1, source_target_pairs={{0,2},{1,3},{2,4},{3,5},{4,6},{5,7},{6,0},{7,1},{8,10},{9,11},{10,... | collective-permute-start | bytes 24584 | tf_op jit(solution)/shard_map/ppermute | solution.py:280
  51.6 4.3 %collective-permute-start.6 = (bf16[8,512]{1,0:T(8,128)(2,1)S(1)}, bf16[8,512]{1,0:T(8,128)(2,1)S(1)}, u32[]{:S(2)}, u32[]{:S(2)}) collective-permute-start(bf16[8,512]{1,0:T(8,128)(2,1)S(1)} %get-tuple-element.22), channel_id=1, source_target_pairs={{0,6},{1,7},{2,0},{3,1},{4,2},{5,3},{6,4},{7,5},{8,14},{9,15},{10,... | collective-permute-start | bytes 24584 | tf_op jit(solution)/shard_map/ppermute | solution.py:280

commit v5 on v4

--- a/solution.py
+++ b/solution.py
@@ -19,9 +19,41 @@
         copies_ref[j] = query_ref[...]
 
 
+def plan_kernel(
+    owner_ref, index_ref, length_ref, row_ref, place_ref, limit_ref, sent_id_ref, local_id_ref,
+    used_count,
+):
+    slots, lanes = place_ref.shape
+    row_requests = row_ref.shape[0] // 8
+    n_inst = ring_y * row_requests // 8
+    block_len = 256
+    my_row = lax.axis_index("y")
+    me = lax.axis_index(inst)
+    lane = lax.broadcasted_iota(jnp.int32, (1, lanes), 1)
+    for j in range(n_inst):
+        used_count[j] = 0
+    for p in range(slots):
+        owner = owner_ref[p]
+        holder = jnp.maximum(owner, 0)
+        home = holder // 8
+        back = lax.rem(my_row + ring_y - holder // row_requests, ring_y)
+        source = back * row_requests + lax.rem(holder, row_requests)
+        foreign = (owner >= 0) & (home != me)
+        local = (owner >= 0) & (home == me)
+        rank = used_count[home]
+        used_count[home] = rank + foreign.astype(jnp.int32)
+        place = jnp.where(foreign, home * lent_slots + rank, n_inst * lent_slots)
+        limit = jnp.where(owner >= 0, length_ref[holder] - index_ref[p] * block_len, 0)
+        request = (holder % 8).astype(f32)
+        place_ref[p : p + 1, :] = jnp.where(lane == 0, source, place)
+        limit_ref[p : p + 1, :] = jnp.full((1, lanes), limit, jnp.int32)
+        sent_id_ref[p : p + 1, :] = jnp.full((1, lanes), request, f32)
+        local_id_ref[p : p + 1, :] = jnp.full((1, lanes), jnp.where(local, request, -1.0), f32)
+
+
 def attend_kernel(
-    owner_ref, index_ref, length_ref, row0_ref, row2_ref, row3_ref, row1_ref, key_ref, value_ref,
-    sent_ref, local_out_ref, local_note_ref, entry_out, entry_note, used_count,
+    place_ref, limit_ref, sent_id_ref, local_id_ref, row0_ref, row2_ref, row3_ref, row1_ref,
+    key_ref, value_ref, sent_ref, local_out_ref, local_note_ref, entry_out, entry_note,
 ):
     slots, block_len, head_dim = key_ref.shape
     heads = 8
@@ -30,8 +62,6 @@
     n_inst = ring_y * row_requests // 8
     spare = n_inst * lent_slots
     scale = head_dim ** (-0.5)
-    my_row = lax.axis_index("y")
-    me = lax.axis_index(inst)
     token = lax.broadcasted_iota(jnp.int32, (heads, block_len), 1)
     lane = lax.broadcasted_iota(jnp.int32, (heads, head_dim), 1)
     kind = lane % 4
@@ -41,27 +71,22 @@
     for e in range(spare):
         entry_out[e] = jnp.zeros((heads, head_dim), f32)
         entry_note[e] = blank
-    for j in range(n_inst):
-        used_count[j] = 0
-
-    owners = [owner_ref[p] for p in range(slots)]
-    holders = [jnp.maximum(o, 0) for o in owners]
+
     scores = []
     for p in range(slots):
-        back = lax.rem(my_row + ring_y - holders[p] // row_requests, ring_y)
-        at = pl.ds(pl.multiple_of((lax.rem(holders[p], row_requests) // 2) * 16, 16), 16)
+        source = place_ref[p, 0]
+        at = pl.ds(pl.multiple_of((lax.rem(source, row_requests) // 2) * 16, 16), 16)
         pair = row_refs[0][at, :]
         for k in range(1, ring_y):
-            pair = jnp.where(back == k, row_refs[k][at, :], pair)
+            pair = jnp.where(source // row_requests == k, row_refs[k][at, :], pair)
         both = lax.dot_general(
             pair, key_ref[p], (((1,), (1,)), ((), ())), preferred_element_type=f32
         )
-        scores.append(jnp.where(holders[p] % 2 == 1, both[heads:], both[:heads]) * scale)
+        scores.append(jnp.where(source % 2 == 1, both[heads:], both[:heads]) * scale)
     notes = []
     for p in range(slots):
-        limit = jnp.where(
-            owners[p] >= 0, length_ref[holders[p]] - index_ref[p] * block_len, 0
-        )
+        limit = jnp.broadcast_to(limit_ref[p : p + 1, :], (heads, head_dim))
+        limit = jnp.concatenate([limit] * (block_len // head_dim), axis=1)
         live = token < limit
         score = jnp.where(live, scores[p], masked_score)
         top = jnp.max(score, axis=1, keepdims=True)
@@ -69,19 +94,13 @@
         weight = jnp.where(live, jnp.exp(score - top), 0.0).astype(bf16)
         total = jnp.sum(weight.astype(f32), axis=1, keepdims=True)
         out = jnp.dot(weight, value_ref[p], preferred_element_type=f32)
-        home = holders[p] // 8
-        request = (holders[p] % 8).astype(f32)
-        foreign = (owners[p] >= 0) & (home != me)
-        local = (owners[p] >= 0) & (home == me)
-        rank = used_count[home]
-        used_count[home] = rank + foreign.astype(jnp.int32)
-        place = jnp.where(foreign, home * lent_slots + rank, spare)
+        place = place_ref[p, 1]
         high = total.astype(bf16).astype(f32)
         note = jnp.where(kind == 0, top, jnp.where(kind == 1, high, total - high))
         entry_out[place] = out
-        entry_note[place] = jnp.where(kind == 3, request, note)
+        entry_note[place] = jnp.where(kind == 3, sent_id_ref[p : p + 1, :], note)
         local_out_ref[p] = out
-        notes.append(jnp.where(kind == 3, jnp.where(local, request, -1.0), note))
+        notes.append(jnp.where(kind == 3, local_id_ref[p : p + 1, :], note))
         if p % 4 == 3:
             a, b, c, d = notes[p - 3 : p + 1]
             local_note_ref[p // 4] = jnp.where(
@@ -217,6 +236,17 @@
     for k in (1, 3, 2):
         pairs = [(i, (i + k) % ring_y) for i in range(ring_y)]
         from_rows[k] = lax.ppermute(row, "y", pairs)
+    plan = pl.pallas_call(
+        plan_kernel,
+        out_shape=(shape((slot_count, head_dim), jnp.int32),) * 2
+        + (shape((slot_count, head_dim), f32),) * 2,
+        in_specs=smem(3) + [pl.BlockSpec(memory_space=pl.ANY)],
+        out_specs=tuple(vmem(4)),
+        scratch_shapes=[pltpu.SMEM((n_inst,), jnp.int32)],
+        compiler_params=params,
+        cost_estimate=pl.CostEstimate(flops=2_000_000_000, bytes_accessed=100_000, transcendentals=0),
+        name="plan",
+    )(block_owner, block_index, lengths, row)
     keys = key_cache.reshape(slot_count, block_len, head_dim)
     values = value_cache.reshape(slot_count, block_len, head_dim)
     sent_rows = (lent_slots + 1) * heads_dev
@@ -227,16 +257,15 @@
             shape((slot_count, heads_dev, head_dim), f32),
             shape((slot_count // lent_slots, heads_dev, head_dim), f32),
         ),
-        in_specs=smem(3) + vmem(6),
+        in_specs=vmem(10),
         out_specs=tuple(vmem(3)),
         scratch_shapes=[
             pltpu.VMEM((n_inst * lent_slots + 1, heads_dev, head_dim), f32),
             pltpu.VMEM((n_inst * lent_slots + 1, heads_dev, head_dim), f32),
-            pltpu.SMEM((n_inst,), jnp.int32),
         ],
         compiler_params=params,
         name="attend",
-    )(block_owner, block_index, lengths, *[from_rows[k] for k in (0, 2, 3, 1)], keys, values)
+    )(*plan, *[from_rows[k] for k in (0, 2, 3, 1)], keys, values)
     got = lax.all_to_all(
         sent.reshape(n_inst, sent_rows, head_dim), inst, 0, 0, tiled=True
     ).reshape(n_inst * sent_rows, head_dim)

time: 57.2 us -> 56.4 us (0.986)
  waiting for transfers between devices: 6.67 us -> 5.66 us
    ppermute x3, waiting for transfers between devices: 4.49 us -> 3.48 us  [body(): from_rows[k] = lax.ppermute(row, 'y', pairs)]
    pallas_call x0 -> x1, Pallas kernels: none -> 0.99 us  [body(): pl.pallas_call(plan_kernel, out_shape=(shape((slot_count, head_dim), jnp....]
  transfers between devices with their start and end apart: 7 -> 7, of which waited for: 4 -> 4; matrix products, arithmetic and copies ran while one was open for 0% -> 0% of each run, Pallas kernels for 1% -> 3%
where the time goes in v5:
time: 56.4 us; the launch traced here: 55.7 us
  blocking collectives  33.2 us (59%)
  starting transfers between devices  11.6 us (21%)
  waiting for transfers between devices  5.66 us (10%)
  Pallas kernels  3.91 us (7%)
  local copies, waits for them, and re-layouts  0.75 us (1%)
  other arithmetic  0.61 us (1%)
    all_to_all x1, blocking collectives, body(): lax.all_to_all(sent.reshape(n_inst, sent_rows, head_dim), inst, 0, 0, til...  17.2 us
    all_to_all x1, blocking collectives, body(): lax.all_to_all(copies, 'z', 0, 0, tiled=True)  15.9 us
    ppermute x3, starting transfers between devices, body(): total = total + lax.ppermute(parts[k - 1], 'tp', pairs).astype(f32)  6.35 us
    ppermute x3, starting transfers between devices, body(): from_rows[k] = lax.ppermute(row, 'y', pairs)  5.22 us
    ppermute x3, waiting for transfers between devices, body(): from_rows[k] = lax.ppermute(row, 'y', pairs)  3.48 us
    ppermute x3, waiting for transfers between devices, body(): total = total + lax.ppermute(parts[k - 1], 'tp', pairs).astype(f32)  1.63 us
    pallas_call x1, Pallas kernels, body(): pl.pallas_call(attend_kernel, out_shape=(shape((n_inst * sent_rows, head_...  1.2 us
  transfers between devices with their start and end apart: 7, of which 4 were waited for; matrix products, arithmetic and copies ran while one was open for 0% of the time, Pallas kernels for 3%

profile of v5, /device:TPU:32, one launch (start us, length us, event | category | flops | bytes accessed | tf_op | source)
XLA Modules:
  0.0 55.7 jit_solution(7554555683857564954)
XLA Ops:
  0.0 0.7 %copy-done.3 = bf16[8,8,128]{2,1,0:T(8,128)(2,1)S(1)} copy-done((bf16[8,8,128]{2,1,0:T(8,128)(2,1)S(1)}, bf16[8,8,128]{2,1,0:T(8,128)(2,1)}, u32[]{:S(2)}) %copy-start.3) | copy-done | bytes 16408
  0.7 15.9 %all_to_all.10 = bf16[8,64,128]{2,1,0:T(8,128)(2,1)S(1)} all-to-all(bf16[8,64,128]{2,1,0:T(8,128)(2,1)S(1)} %copies.1), channel_id=1, replica_groups=mesh['y'=4,'z'=8,'tp'=8] {'z'}, dimensions={0} | all-to-all | bytes 262144 | tf_op jit(solution)/shard_map/all_to_all | solution.py:234
  16.7 1.6 %collective-permute-start.2 = (bf16[512,128]{1,0:T(8,128)(2,1)S(1)}, bf16[512,128]{1,0:T(8,128)(2,1)S(1)}, u32[]{:S(2)}, u32[]{:S(2)}) collective-permute-start(bf16[512,128]{1,0:T(8,128)(2,1)S(1)} %bitcast.11), channel_id=1, source_target_pairs={{0,64},{64,128},{128,192},{192,0},{1,65},{65,129},{129,193},{193,1... | collective-permute-start | bytes 393224 | tf_op jit(solution)/shard_map/ppermute | solution.py:238
  18.3 1.7 %collective-permute-start.1 = (bf16[512,128]{1,0:T(8,128)(2,1)S(1)}, bf16[512,128]{1,0:T(8,128)(2,1)S(1)}, u32[]{:S(2)}, u32[]{:S(2)}) collective-permute-start(bf16[512,128]{1,0:T(8,128)(2,1)S(1)} %bitcast.12), channel_id=1, source_target_pairs={{0,192},{64,0},{128,64},{192,128},{1,193},{65,1},{129,65},{193,129... | collective-permute-start | bytes 393224 | tf_op jit(solution)/shard_map/ppermute | solution.py:238
  19.9 2.0 %collective-permute-start = (bf16[512,128]{1,0:T(8,128)(2,1)S(1)}, bf16[512,128]{1,0:T(8,128)(2,1)S(1)}, u32[]{:S(2)}, u32[]{:S(2)}) collective-permute-start(bf16[512,128]{1,0:T(8,128)(2,1)S(1)} %bitcast.13), channel_id=1, source_target_pairs={{0,128},{64,192},{128,0},{192,64},{1,129},{65,193},{129,1},{193,65... | collective-permute-start | bytes 393224 | tf_op jit(solution)/shard_map/ppermute | solution.py:238
  21.9 0.0 copy-done.7
  21.9 0.0 copy-done.8
  21.9 0.0 copy-done.9
  21.9 1.0 %plan.1 = (s32[32,128]{1,0:T(8,128)S(1)}, s32[32,128]{1,0:T(8,128)S(1)}, f32[32,128]{1,0:T(8,128)S(1)}, f32[32,128]{1,0:T(8,128)S(1)}) custom-call(s32[32]{0:T(128)S(1)} %copy-done.8, s32[32]{0:T(128)S(1)} %copy-done.9, s32[256]{0:T(256)S(1)} %copy-done.7, bf16[512,128]{1,0:T(8,128)(2,1)S(1)} %bitcast.14), custom_call_target="tpu_custom_call" | custom-call | flops 2000000000 | bytes 100000 | tf_op jit(solution)/shard_map/plan/pallas_call | solution.py:239
  22.9 1.1 %collective-permute-done.2.row1_ref = bf16[512,128]{1,0:T(8,128)(2,1)S(1)} collective-permute-done((bf16[512,128]{1,0:T(8,128)(2,1)S(1)}, bf16[512,128]{1,0:T(8,128)(2,1)S(1)}, u32[]{:S(2)}, u32[]{:S(2)}) %collective-permute-start.2) | collective-permute-done | bytes 131104 | tf_op jit(solution)/shard_map/ppermute | solution.py:238
  24.0 0.0 collective-permute-done.1.row3_ref
  24.0 2.4 %collective-permute-done.row2_ref = bf16[512,128]{1,0:T(8,128)(2,1)S(1)} collective-permute-done((bf16[512,128]{1,0:T(8,128)(2,1)S(1)}, bf16[512,128]{1,0:T(8,128)(2,1)S(1)}, u32[]{:S(2)}, u32[]{:S(2)}) %collective-permute-start) | collective-permute-done | bytes 131104 | tf_op jit(solution)/shard_map/ppermute | solution.py:238
  26.4 0.0 copy-done.1
  26.4 0.0 copy-done.2
  26.4 0.0 copy-start.6
  26.4 1.2 %attend.1 = (bf16[1280,128]{1,0:T(8,128)(2,1)S(1)}, f32[32,8,128]{2,1,0:T(8,128)S(1)}, f32[8,8,128]{2,1,0:T(8,128)S(1)}) custom-call(s32[32,128]{1,0:T(8,128)S(1)} %get-tuple-element.18.place_ref, s32[32,128]{1,0:T(8,128)S(1)} %get-tuple-element.19.limit_ref, f32[32,128]{1,0:T(8,128)S(1)} %get-tuple-element.20.sent_id_ref, ...), custom_call_target="tpu_custom_call" | custom-call | tf_op jit(solution)/shard_map/attend/pallas_call | solution.py:253
  27.6 17.2 %all_to_all.11 = bf16[32,40,128]{2,1,0:T(8,128)(2,1)S(1)} all-to-all(bf16[32,40,128]{2,1,0:T(8,128)(2,1)S(1)} %bitcast.16), channel_id=1, replica_groups=mesh['y'=4,'z'=8,'tp'=8] {'y','z'}, dimensions={0} | all-to-all | bytes 655360 | tf_op jit(solution)/shard_map/all_to_all | solution.py:269
  44.9 0.0 copy-done
  44.9 0.0 copy-done.4
  44.9 0.0 copy-done.5
  44.9 0.0 copy-done.6
  44.9 1.0 %merge.1 = (bf16[8,1024]{1,0:T(8,128)(2,1)S(1)}, bf16[8,2048]{1,0:T(8,128)(2,1)S(1)}) custom-call(bf16[1280,128]{1,0:T(8,128)(2,1)S(1)} %bitcast.10, f32[32,8,128]{2,1,0:T(8,128)S(1)} %get-tuple-element.23.local_out_ref, f32[8,8,128]{2,1,0:T(8,128)S(1)} %get-tuple-element.24.local_note_ref, bf16[64,128]{1,0:T(8,128)(2,1)S(1)} %bitcast.18, ...), custom_call_target="tpu_custom_call" | custom-call | tf_op jit(solution)/shard_map/merge/pallas_call | solution.py:272
  45.9 0.0 collective-permute-start.3
  45.9 0.7 %project.1.keep_ref = f32[8,2048]{1,0:T(8,128)S(1)} custom-call(bf16[8,1024]{1,0:T(8,128)(2,1)S(1)} %get-tuple-element.25.attended_ref, bf16[1024,4096]{1,0:T(8,128)(2,1)S(1)} %copy-done), custom_call_target="tpu_custom_call" | custom-call | flops 200000000 | bytes 4000000 | tf_op jit(solution)/shard_map/project/pallas_call | solution.py:288
  46.6 0.6 collective-permute-done.3.got_ref
  47.2 3.1 %collective-permute-start.4 = (bf16[8,512]{1,0:T(8,128)(2,1)S(1)}, bf16[8,512]{1,0:T(8,128)(2,1)S(1)}, u32[]{:S(2)}, u32[]{:S(2)}) collective-permute-start(bf16[8,512]{1,0:T(8,128)(2,1)S(1)} %get-tuple-element.28), channel_id=1, source_target_pairs={{0,4},{1,5},{2,6},{3,7},{4,0},{5,1},{6,2},{7,3},{8,12},{9,13},{10,... | collective-permute-start | bytes 24584 | tf_op jit(solution)/shard_map/ppermute | solution.py:309
  50.3 0.6 %collective-permute-start.5 = (bf16[8,512]{1,0:T(8,128)(2,1)S(1)}, bf16[8,512]{1,0:T(8,128)(2,1)S(1)}, u32[]{:S(2)}, u32[]{:S(2)}) collective-permute-start(bf16[8,512]{1,0:T(8,128)(2,1)S(1)} %get-tuple-element.29), channel_id=1, source_target_pairs={{0,2},{1,3},{2,4},{3,5},{4,6},{5,7},{6,0},{7,1},{8,10},{9,11},{10,... | collective-permute-start | bytes 24584 | tf_op jit(solution)/shard_map/ppermute | solution.py:309
  50.9 2.6 %collective-permute-start.6 = (bf16[8,512]{1,0:T(8,128)(2,1)S(1)}, bf16[8,512]{1,0:T(8,128)(2,1)S(1)}, u32[]{:S(2)}, u32[]{:S(2)}) collective-permute-start(bf16[8,512]{1,0:T(8,128)(2,1)S(1)} %get-tuple-element.30), channel_id=1, source_target_pairs={{0,6},{1,7},{2,0},{3,1},{4,2},{5,3},{6,4},{7,5},{8,14},{9,15},{10,... | collective-permute-start | bytes 24584 | tf_op jit(solution)/shard_map/ppermute | solution.py:309
  53.5 0.0 collective-permute-done.4
  53.5 1.6 %collective-permute-done.5 = bf16[8,512]{1,0:T(8,128)(2,1)S(1)} collective-permute-done((bf16[8,512]{1,0:T(8,128)(2,1)S(1)}, bf16[8,512]{1,0:T(8,128)(2,1)S(1)}, u32[]{:S(2)}, u32[]{:S(2)}) %collective-permute-start.5) | collective-permute-done | bytes 8224 | tf_op jit(solution)/shard_map/ppermute | solution.py:309
  55.1 0.0 collective-permute-done.6
  55.1 0.6 %add_convert_fusion = bf16[8,512]{1,0:T(8,128)(2,1)} fusion(bf16[8,512]{1,0:T(8,128)(2,1)S(1)} %collective-permute-done.6, bf16[8,512]{1,0:T(8,128)(2,1)S(1)} %collective-permute-done.5, f32[8,512]{1,0:T(8,128)S(1)} %get-tuple-element.27, bf16[8,512]{1,0:T(8,128)(2,1)S(1)} %collective-permute-done.4), kind=kLoop, calls=%fused_computation | loop fusion | flops 28672 | bytes 49152 | tf_op jit(solution)/shard_map/convert_element_type | solution.py:310
  (11 shorter events, 0.0 us)
Async XLA Ops:
  0.0 0.7 %copy-start.3 = (bf16[8,8,128]{2,1,0:T(8,128)(2,1)S(1)}, bf16[8,8,128]{2,1,0:T(8,128)(2,1)}, u32[]{:S(2)}) copy-start(bf16[8,8,128]{2,1,0:T(8,128)(2,1)} %param.9) | copy-start | bytes 49156
  0.7 21.2 %copy-start.7 = (s32[256]{0:T(256)S(1)}, s32[256]{0:T(256)}, u32[]{:S(2)}) copy-start(s32[256]{0:T(256)} %length_ref.1) | copy-start | bytes 3076
  0.7 21.2 %copy-start.8 = (s32[32]{0:T(128)S(1)}, s32[32]{0:T(128)}, u32[]{:S(2)}) copy-start(s32[32]{0:T(128)} %owner_ref.1) | copy-start | bytes 388
  0.7 21.2 %copy-start.9 = (s32[32]{0:T(128)S(1)}, s32[32]{0:T(128)}, u32[]{:S(2)}) copy-start(s32[32]{0:T(128)} %index_ref.1) | copy-start | bytes 388
  16.7 9.7 %copy-start.1 = (bf16[32,256,1,128]{3,1,2,0:T(8,128)(2,1)S(1)}, bf16[32,256,1,128]{3,1,2,0:T(8,128)(2,1)}, u32[]{:S(2)}) copy-start(bf16[32,256,1,128]{3,1,2,0:T(8,128)(2,1)} %param.12) | copy-start | bytes 6291460
  16.7 9.7 %copy-start.2 = (bf16[32,256,1,128]{3,1,2,0:T(8,128)(2,1)S(1)}, bf16[32,256,1,128]{3,1,2,0:T(8,128)(2,1)}, u32[]{:S(2)}) copy-start(bf16[32,256,1,128]{3,1,2,0:T(8,128)(2,1)} %param.13) | copy-start | bytes 6291460
  16.7 7.3 %collective-permute-start.2 = (bf16[512,128]{1,0:T(8,128)(2,1)S(1)}, bf16[512,128]{1,0:T(8,128)(2,1)S(1)}, u32[]{:S(2)}, u32[]{:S(2)}) collective-permute-start(bf16[512,128]{1,0:T(8,128)(2,1)S(1)} %bitcast.11), channel_id=1, source_target_pairs={{0,64},{64,128},{128,192},{192,0},{1,65},{65,129},{129,193},{193,1... | collective-permute-start | bytes 393224 | tf_op jit(solution)/shard_map/ppermute | solution.py:238
  18.3 5.7 %collective-permute-start.1 = (bf16[512,128]{1,0:T(8,128)(2,1)S(1)}, bf16[512,128]{1,0:T(8,128)(2,1)S(1)}, u32[]{:S(2)}, u32[]{:S(2)}) collective-permute-start(bf16[512,128]{1,0:T(8,128)(2,1)S(1)} %bitcast.12), channel_id=1, source_target_pairs={{0,192},{64,0},{128,64},{192,128},{1,193},{65,1},{129,65},{193,129... | collective-permute-start | bytes 393224 | tf_op jit(solution)/shard_map/ppermute | solution.py:238
  19.9 6.5 %collective-permute-start = (bf16[512,128]{1,0:T(8,128)(2,1)S(1)}, bf16[512,128]{1,0:T(8,128)(2,1)S(1)}, u32[]{:S(2)}, u32[]{:S(2)}) collective-permute-start(bf16[512,128]{1,0:T(8,128)(2,1)S(1)} %bitcast.13), channel_id=1, source_target_pairs={{0,128},{64,192},{128,0},{192,64},{1,129},{65,193},{129,1},{193,65... | collective-permute-start | bytes 393224 | tf_op jit(solution)/shard_map/ppermute | solution.py:238
  21.9 22.9 %copy-start = (bf16[1024,4096]{1,0:T(8,128)(2,1)S(1)}, bf16[1024,4096]{1,0:T(8,128)(2,1)}, u32[]{:S(2)}) copy-start(bf16[1024,4096]{1,0:T(8,128)(2,1)} %weight_ref.3) | copy-start | bytes 25165828
  26.4 18.5 %copy-start.4 = (bf16[8,8,128]{2,1,0:T(8,128)(2,1)S(1)}, bf16[8,8,128]{2,1,0:T(8,128)(2,1)}, u32[]{:S(2)}) copy-start(bf16[8,8,128]{2,1,0:T(8,128)(2,1)} %param.9) | copy-start | bytes 49156
  26.4 18.5 %copy-start.5 = (bf16[8,1,128]{2,0,1:T(8,128)(2,1)S(1)}, bf16[8,1,128]{2,0,1:T(8,128)(2,1)}, u32[]{:S(2)}) copy-start(bf16[8,1,128]{2,0,1:T(8,128)(2,1)} %param.10) | copy-start | bytes 6148
  26.4 18.5 %copy-start.6 = (bf16[8,1,128]{2,0,1:T(8,128)(2,1)S(1)}, bf16[8,1,128]{2,0,1:T(8,128)(2,1)}, u32[]{:S(2)}) copy-start(bf16[8,1,128]{2,0,1:T(8,128)(2,1)} %param.11) | copy-start | bytes 6148
  45.9 1.2 %collective-permute-start.3 = (bf16[8,2048]{1,0:T(8,128)(2,1)S(1)}, bf16[8,2048]{1,0:T(8,128)(2,1)S(1)}, u32[]{:S(2)}, u32[]{:S(2)}) collective-permute-start(bf16[8,2048]{1,0:T(8,128)(2,1)S(1)} %get-tuple-element.26), channel_id=1, source_target_pairs={{0,1},{1,0},{2,3},{3,2},{4,5},{5,4},{6,7},{7,6},{8,9},{9,8},{10,11... | collective-permute-start | bytes 98312 | tf_op jit(solution)/shard_map/ppermute | solution.py:287
  47.2 6.4 %collective-permute-start.4 = (bf16[8,512]{1,0:T(8,128)(2,1)S(1)}, bf16[8,512]{1,0:T(8,128)(2,1)S(1)}, u32[]{:S(2)}, u32[]{:S(2)}) collective-permute-start(bf16[8,512]{1,0:T(8,128)(2,1)S(1)} %get-tuple-element.28), channel_id=1, source_target_pairs={{0,4},{1,5},{2,6},{3,7},{4,0},{5,1},{6,2},{7,3},{8,12},{9,13},{10,... | collective-permute-start | bytes 24584 | tf_op jit(solution)/shard_map/ppermute | solution.py:309
  50.3 4.9 %collective-permute-start.5 = (bf16[8,512]{1,0:T(8,128)(2,1)S(1)}, bf16[8,512]{1,0:T(8,128)(2,1)S(1)}, u32[]{:S(2)}, u32[]{:S(2)}) collective-permute-start(bf16[8,512]{1,0:T(8,128)(2,1)S(1)} %get-tuple-element.29), channel_id=1, source_target_pairs={{0,2},{1,3},{2,4},{3,5},{4,6},{5,7},{6,0},{7,1},{8,10},{9,11},{10,... | collective-permute-start | bytes 24584 | tf_op jit(solution)/shard_map/ppermute | solution.py:309
  50.9 4.3 %collective-permute-start.6 = (bf16[8,512]{1,0:T(8,128)(2,1)S(1)}, bf16[8,512]{1,0:T(8,128)(2,1)S(1)}, u32[]{:S(2)}, u32[]{:S(2)}) collective-permute-start(bf16[8,512]{1,0:T(8,128)(2,1)S(1)} %get-tuple-element.30), channel_id=1, source_target_pairs={{0,6},{1,7},{2,0},{3,1},{4,2},{5,3},{6,4},{7,5},{8,14},{9,15},{10,... | collective-permute-start | bytes 24584 | tf_op jit(solution)/shard_map/ppermute | solution.py:309

commit v6 on v5

--- a/solution.py
+++ b/solution.py
@@ -304,7 +304,7 @@
         name="split",
     )(keep, from_core)
     total = own
-    for k in (2, 1, 3):
+    for k in (1, 2, 3):
         pairs = [(i, (i + 2 * k) % n_tp) for i in range(n_tp)]
         total = total + lax.ppermute(parts[k - 1], "tp", pairs).astype(f32)
     return total.astype(bf16)

time: 56.4 us -> 55.9 us (level)
  starting transfers between devices: 11.6 us -> 11 us
  waiting for transfers between devices: 5.66 us -> 6.25 us
    ppermute x3, starting transfers between devices: 6.35 us -> 5.73 us  [body(): total = total + lax.ppermute(parts[k - 1], 'tp', pairs).astype(f32)]
    ppermute x3, waiting for transfers between devices: 1.63 us -> 2.21 us  [body(): total = total + lax.ppermute(parts[k - 1], 'tp', pairs).astype(f32)]
  transfers between devices with their start and end apart: 7 -> 7, of which waited for: 4 -> 5; matrix products, arithmetic and copies ran while one was open for 0% -> 0% of each run, Pallas kernels for 3% -> 3%
where the time goes in v6:
time: 55.9 us; the launch traced here: 55.7 us
  blocking collectives  33.2 us (59%)
  starting transfers between devices  11 us (20%)
  waiting for transfers between devices  6.25 us (11%)
  Pallas kernels  3.92 us (7%)
  local copies, waits for them, and re-layouts  0.75 us (1%)
  other arithmetic  0.61 us (1%)
    all_to_all x1, blocking collectives, body(): lax.all_to_all(sent.reshape(n_inst, sent_rows, head_dim), inst, 0, 0, til...  17.2 us
    all_to_all x1, blocking collectives, body(): lax.all_to_all(copies, 'z', 0, 0, tiled=True)  15.9 us
    ppermute x3, starting transfers between devices, body(): total = total + lax.ppermute(parts[k - 1], 'tp', pairs).astype(f32)  5.73 us
    ppermute x3, starting transfers between devices, body(): from_rows[k] = lax.ppermute(row, 'y', pairs)  5.22 us
    ppermute x3, waiting for transfers between devices, body(): from_rows[k] = lax.ppermute(row, 'y', pairs)  3.48 us
    ppermute x3, waiting for transfers between devices, body(): total = total + lax.ppermute(parts[k - 1], 'tp', pairs).astype(f32)  2.21 us
    pallas_call x1, Pallas kernels, body(): pl.pallas_call(attend_kernel, out_shape=(shape((n_inst * sent_rows, head_...  1.2 us
  transfers between devices with their start and end apart: 7, of which 5 were waited for; matrix products, arithmetic and copies ran while one was open for 0% of the time, Pallas kernels for 3%

profile of v6, /device:TPU:32, one launch (start us, length us, event | category | flops | bytes accessed | tf_op | source)
XLA Modules:
  0.0 55.7 jit_solution(3623867688465423917)
XLA Ops:
  0.0 0.7 %copy-done.3 = bf16[8,8,128]{2,1,0:T(8,128)(2,1)S(1)} copy-done((bf16[8,8,128]{2,1,0:T(8,128)(2,1)S(1)}, bf16[8,8,128]{2,1,0:T(8,128)(2,1)}, u32[]{:S(2)}) %copy-start.3) | copy-done | bytes 16408
  0.7 15.9 %all_to_all.10 = bf16[8,64,128]{2,1,0:T(8,128)(2,1)S(1)} all-to-all(bf16[8,64,128]{2,1,0:T(8,128)(2,1)S(1)} %copies.1), channel_id=1, replica_groups=mesh['y'=4,'z'=8,'tp'=8] {'z'}, dimensions={0} | all-to-all | bytes 262144 | tf_op jit(solution)/shard_map/all_to_all | solution.py:234
  16.7 1.6 %collective-permute-start.2 = (bf16[512,128]{1,0:T(8,128)(2,1)S(1)}, bf16[512,128]{1,0:T(8,128)(2,1)S(1)}, u32[]{:S(2)}, u32[]{:S(2)}) collective-permute-start(bf16[512,128]{1,0:T(8,128)(2,1)S(1)} %bitcast.11), channel_id=1, source_target_pairs={{0,64},{64,128},{128,192},{192,0},{1,65},{65,129},{129,193},{193,1... | collective-permute-start | bytes 393224 | tf_op jit(solution)/shard_map/ppermute | solution.py:238
  18.3 1.7 %collective-permute-start.1 = (bf16[512,128]{1,0:T(8,128)(2,1)S(1)}, bf16[512,128]{1,0:T(8,128)(2,1)S(1)}, u32[]{:S(2)}, u32[]{:S(2)}) collective-permute-start(bf16[512,128]{1,0:T(8,128)(2,1)S(1)} %bitcast.12), channel_id=1, source_target_pairs={{0,192},{64,0},{128,64},{192,128},{1,193},{65,1},{129,65},{193,129... | collective-permute-start | bytes 393224 | tf_op jit(solution)/shard_map/ppermute | solution.py:238
  19.9 2.0 %collective-permute-start = (bf16[512,128]{1,0:T(8,128)(2,1)S(1)}, bf16[512,128]{1,0:T(8,128)(2,1)S(1)}, u32[]{:S(2)}, u32[]{:S(2)}) collective-permute-start(bf16[512,128]{1,0:T(8,128)(2,1)S(1)} %bitcast.13), channel_id=1, source_target_pairs={{0,128},{64,192},{128,0},{192,64},{1,129},{65,193},{129,1},{193,65... | collective-permute-start | bytes 393224 | tf_op jit(solution)/shard_map/ppermute | solution.py:238
  21.9 0.0 copy-done.7
  21.9 0.0 copy-done.8
  21.9 0.0 copy-done.9
  21.9 1.0 %plan.1 = (s32[32,128]{1,0:T(8,128)S(1)}, s32[32,128]{1,0:T(8,128)S(1)}, f32[32,128]{1,0:T(8,128)S(1)}, f32[32,128]{1,0:T(8,128)S(1)}) custom-call(s32[32]{0:T(128)S(1)} %copy-done.8, s32[32]{0:T(128)S(1)} %copy-done.9, s32[256]{0:T(256)S(1)} %copy-done.7, bf16[512,128]{1,0:T(8,128)(2,1)S(1)} %bitcast.14), custom_call_target="tpu_custom_call" | custom-call | flops 2000000000 | bytes 100000 | tf_op jit(solution)/shard_map/plan/pallas_call | solution.py:239
  22.9 1.1 %collective-permute-done.2.row1_ref = bf16[512,128]{1,0:T(8,128)(2,1)S(1)} collective-permute-done((bf16[512,128]{1,0:T(8,128)(2,1)S(1)}, bf16[512,128]{1,0:T(8,128)(2,1)S(1)}, u32[]{:S(2)}, u32[]{:S(2)}) %collective-permute-start.2) | collective-permute-done | bytes 131104 | tf_op jit(solution)/shard_map/ppermute | solution.py:238
  24.0 0.0 collective-permute-done.1.row3_ref
  24.0 2.4 %collective-permute-done.row2_ref = bf16[512,128]{1,0:T(8,128)(2,1)S(1)} collective-permute-done((bf16[512,128]{1,0:T(8,128)(2,1)S(1)}, bf16[512,128]{1,0:T(8,128)(2,1)S(1)}, u32[]{:S(2)}, u32[]{:S(2)}) %collective-permute-start) | collective-permute-done | bytes 131104 | tf_op jit(solution)/shard_map/ppermute | solution.py:238
  26.4 0.0 copy-done.1
  26.4 0.0 copy-done.2
  26.4 0.0 copy-start.6
  26.4 1.2 %attend.1 = (bf16[1280,128]{1,0:T(8,128)(2,1)S(1)}, f32[32,8,128]{2,1,0:T(8,128)S(1)}, f32[8,8,128]{2,1,0:T(8,128)S(1)}) custom-call(s32[32,128]{1,0:T(8,128)S(1)} %get-tuple-element.18.place_ref, s32[32,128]{1,0:T(8,128)S(1)} %get-tuple-element.19.limit_ref, f32[32,128]{1,0:T(8,128)S(1)} %get-tuple-element.20.sent_id_ref, ...), custom_call_target="tpu_custom_call" | custom-call | tf_op jit(solution)/shard_map/attend/pallas_call | solution.py:253
  27.6 17.2 %all_to_all.11 = bf16[32,40,128]{2,1,0:T(8,128)(2,1)S(1)} all-to-all(bf16[32,40,128]{2,1,0:T(8,128)(2,1)S(1)} %bitcast.16), channel_id=1, replica_groups=mesh['y'=4,'z'=8,'tp'=8] {'y','z'}, dimensions={0} | all-to-all | bytes 655360 | tf_op jit(solution)/shard_map/all_to_all | solution.py:269
  44.9 0.0 copy-done
  44.9 0.0 copy-done.4
  44.9 0.0 copy-done.5
  44.9 0.0 copy-done.6
  44.9 1.0 %merge.1 = (bf16[8,1024]{1,0:T(8,128)(2,1)S(1)}, bf16[8,2048]{1,0:T(8,128)(2,1)S(1)}) custom-call(bf16[1280,128]{1,0:T(8,128)(2,1)S(1)} %bitcast.10, f32[32,8,128]{2,1,0:T(8,128)S(1)} %get-tuple-element.23.local_out_ref, f32[8,8,128]{2,1,0:T(8,128)S(1)} %get-tuple-element.24.local_note_ref, bf16[64,128]{1,0:T(8,128)(2,1)S(1)} %bitcast.18, ...), custom_call_target="tpu_custom_call" | custom-call | tf_op jit(solution)/shard_map/merge/pallas_call | solution.py:272
  45.9 0.0 collective-permute-start.3
  45.9 0.7 %project.1.keep_ref = f32[8,2048]{1,0:T(8,128)S(1)} custom-call(bf16[8,1024]{1,0:T(8,128)(2,1)S(1)} %get-tuple-element.25.attended_ref, bf16[1024,4096]{1,0:T(8,128)(2,1)S(1)} %copy-done), custom_call_target="tpu_custom_call" | custom-call | flops 200000000 | bytes 4000000 | tf_op jit(solution)/shard_map/project/pallas_call | solution.py:288
  46.6 0.6 collective-permute-done.3.got_ref
  47.2 1.6 %collective-permute-start.4 = (bf16[8,512]{1,0:T(8,128)(2,1)S(1)}, bf16[8,512]{1,0:T(8,128)(2,1)S(1)}, u32[]{:S(2)}, u32[]{:S(2)}) collective-permute-start(bf16[8,512]{1,0:T(8,128)(2,1)S(1)} %get-tuple-element.28), channel_id=1, source_target_pairs={{0,2},{1,3},{2,4},{3,5},{4,6},{5,7},{6,0},{7,1},{8,10},{9,11},{10,... | collective-permute-start | bytes 24584 | tf_op jit(solution)/shard_map/ppermute | solution.py:309
  48.7 2.7 %collective-permute-start.5 = (bf16[8,512]{1,0:T(8,128)(2,1)S(1)}, bf16[8,512]{1,0:T(8,128)(2,1)S(1)}, u32[]{:S(2)}, u32[]{:S(2)}) collective-permute-start(bf16[8,512]{1,0:T(8,128)(2,1)S(1)} %get-tuple-element.29), channel_id=1, source_target_pairs={{0,4},{1,5},{2,6},{3,7},{4,0},{5,1},{6,2},{7,3},{8,12},{9,13},{10,... | collective-permute-start | bytes 24584 | tf_op jit(solution)/shard_map/ppermute | solution.py:309
  51.5 1.4 %collective-permute-start.6 = (bf16[8,512]{1,0:T(8,128)(2,1)S(1)}, bf16[8,512]{1,0:T(8,128)(2,1)S(1)}, u32[]{:S(2)}, u32[]{:S(2)}) collective-permute-start(bf16[8,512]{1,0:T(8,128)(2,1)S(1)} %get-tuple-element.30), channel_id=1, source_target_pairs={{0,6},{1,7},{2,0},{3,1},{4,2},{5,3},{6,4},{7,5},{8,14},{9,15},{10,... | collective-permute-start | bytes 24584 | tf_op jit(solution)/shard_map/ppermute | solution.py:309
  52.9 0.0 collective-permute-done.4
  52.9 1.0 %collective-permute-done.5 = bf16[8,512]{1,0:T(8,128)(2,1)S(1)} collective-permute-done((bf16[8,512]{1,0:T(8,128)(2,1)S(1)}, bf16[8,512]{1,0:T(8,128)(2,1)S(1)}, u32[]{:S(2)}, u32[]{:S(2)}) %collective-permute-start.5) | collective-permute-done | bytes 8224 | tf_op jit(solution)/shard_map/ppermute | solution.py:309
  53.9 1.2 %collective-permute-done.6 = bf16[8,512]{1,0:T(8,128)(2,1)S(1)} collective-permute-done((bf16[8,512]{1,0:T(8,128)(2,1)S(1)}, bf16[8,512]{1,0:T(8,128)(2,1)S(1)}, u32[]{:S(2)}, u32[]{:S(2)}) %collective-permute-start.6) | collective-permute-done | bytes 8224 | tf_op jit(solution)/shard_map/ppermute | solution.py:309
  55.1 0.6 %add_convert_fusion = bf16[8,512]{1,0:T(8,128)(2,1)} fusion(bf16[8,512]{1,0:T(8,128)(2,1)S(1)} %collective-permute-done.6, bf16[8,512]{1,0:T(8,128)(2,1)S(1)} %collective-permute-done.5, f32[8,512]{1,0:T(8,128)S(1)} %get-tuple-element.27, bf16[8,512]{1,0:T(8,128)(2,1)S(1)} %collective-permute-done.4), kind=kLoop, calls=%fused_computation | loop fusion | flops 28672 | bytes 49152 | tf_op jit(solution)/shard_map/convert_element_type | solution.py:310
  (11 shorter events, 0.0 us)
Async XLA Ops:
  0.0 0.7 %copy-start.3 = (bf16[8,8,128]{2,1,0:T(8,128)(2,1)S(1)}, bf16[8,8,128]{2,1,0:T(8,128)(2,1)}, u32[]{:S(2)}) copy-start(bf16[8,8,128]{2,1,0:T(8,128)(2,1)} %param.9) | copy-start | bytes 49156
  0.7 21.2 %copy-start.7 = (s32[256]{0:T(256)S(1)}, s32[256]{0:T(256)}, u32[]{:S(2)}) copy-start(s32[256]{0:T(256)} %length_ref.1) | copy-start | bytes 3076
  0.7 21.2 %copy-start.8 = (s32[32]{0:T(128)S(1)}, s32[32]{0:T(128)}, u32[]{:S(2)}) copy-start(s32[32]{0:T(128)} %owner_ref.1) | copy-start | bytes 388
  0.7 21.2 %copy-start.9 = (s32[32]{0:T(128)S(1)}, s32[32]{0:T(128)}, u32[]{:S(2)}) copy-start(s32[32]{0:T(128)} %index_ref.1) | copy-start | bytes 388
  16.7 9.7 %copy-start.1 = (bf16[32,256,1,128]{3,1,2,0:T(8,128)(2,1)S(1)}, bf16[32,256,1,128]{3,1,2,0:T(8,128)(2,1)}, u32[]{:S(2)}) copy-start(bf16[32,256,1,128]{3,1,2,0:T(8,128)(2,1)} %param.12) | copy-start | bytes 6291460
  16.7 9.7 %copy-start.2 = (bf16[32,256,1,128]{3,1,2,0:T(8,128)(2,1)S(1)}, bf16[32,256,1,128]{3,1,2,0:T(8,128)(2,1)}, u32[]{:S(2)}) copy-start(bf16[32,256,1,128]{3,1,2,0:T(8,128)(2,1)} %param.13) | copy-start | bytes 6291460
  16.7 7.3 %collective-permute-start.2 = (bf16[512,128]{1,0:T(8,128)(2,1)S(1)}, bf16[512,128]{1,0:T(8,128)(2,1)S(1)}, u32[]{:S(2)}, u32[]{:S(2)}) collective-permute-start(bf16[512,128]{1,0:T(8,128)(2,1)S(1)} %bitcast.11), channel_id=1, source_target_pairs={{0,64},{64,128},{128,192},{192,0},{1,65},{65,129},{129,193},{193,1... | collective-permute-start | bytes 393224 | tf_op jit(solution)/shard_map/ppermute | solution.py:238
  18.3 5.7 %collective-permute-start.1 = (bf16[512,128]{1,0:T(8,128)(2,1)S(1)}, bf16[512,128]{1,0:T(8,128)(2,1)S(1)}, u32[]{:S(2)}, u32[]{:S(2)}) collective-permute-start(bf16[512,128]{1,0:T(8,128)(2,1)S(1)} %bitcast.12), channel_id=1, source_target_pairs={{0,192},{64,0},{128,64},{192,128},{1,193},{65,1},{129,65},{193,129... | collective-permute-start | bytes 393224 | tf_op jit(solution)/shard_map/ppermute | solution.py:238
  19.9 6.5 %collective-permute-start = (bf16[512,128]{1,0:T(8,128)(2,1)S(1)}, bf16[512,128]{1,0:T(8,128)(2,1)S(1)}, u32[]{:S(2)}, u32[]{:S(2)}) collective-permute-start(bf16[512,128]{1,0:T(8,128)(2,1)S(1)} %bitcast.13), channel_id=1, source_target_pairs={{0,128},{64,192},{128,0},{192,64},{1,129},{65,193},{129,1},{193,65... | collective-permute-start | bytes 393224 | tf_op jit(solution)/shard_map/ppermute | solution.py:238
  21.9 22.9 %copy-start = (bf16[1024,4096]{1,0:T(8,128)(2,1)S(1)}, bf16[1024,4096]{1,0:T(8,128)(2,1)}, u32[]{:S(2)}) copy-start(bf16[1024,4096]{1,0:T(8,128)(2,1)} %weight_ref.3) | copy-start | bytes 25165828
  26.4 18.5 %copy-start.4 = (bf16[8,8,128]{2,1,0:T(8,128)(2,1)S(1)}, bf16[8,8,128]{2,1,0:T(8,128)(2,1)}, u32[]{:S(2)}) copy-start(bf16[8,8,128]{2,1,0:T(8,128)(2,1)} %param.9) | copy-start | bytes 49156
  26.4 18.5 %copy-start.5 = (bf16[8,1,128]{2,0,1:T(8,128)(2,1)S(1)}, bf16[8,1,128]{2,0,1:T(8,128)(2,1)}, u32[]{:S(2)}) copy-start(bf16[8,1,128]{2,0,1:T(8,128)(2,1)} %param.10) | copy-start | bytes 6148
  26.4 18.5 %copy-start.6 = (bf16[8,1,128]{2,0,1:T(8,128)(2,1)S(1)}, bf16[8,1,128]{2,0,1:T(8,128)(2,1)}, u32[]{:S(2)}) copy-start(bf16[8,1,128]{2,0,1:T(8,128)(2,1)} %param.11) | copy-start | bytes 6148
  45.9 1.2 %collective-permute-start.3 = (bf16[8,2048]{1,0:T(8,128)(2,1)S(1)}, bf16[8,2048]{1,0:T(8,128)(2,1)S(1)}, u32[]{:S(2)}, u32[]{:S(2)}) collective-permute-start(bf16[8,2048]{1,0:T(8,128)(2,1)S(1)} %get-tuple-element.26), channel_id=1, source_target_pairs={{0,1},{1,0},{2,3},{3,2},{4,5},{5,4},{6,7},{7,6},{8,9},{9,8},{10,11... | collective-permute-start | bytes 98312 | tf_op jit(solution)/shard_map/ppermute | solution.py:287
  47.2 5.7 %collective-permute-start.4 = (bf16[8,512]{1,0:T(8,128)(2,1)S(1)}, bf16[8,512]{1,0:T(8,128)(2,1)S(1)}, u32[]{:S(2)}, u32[]{:S(2)}) collective-permute-start(bf16[8,512]{1,0:T(8,128)(2,1)S(1)} %get-tuple-element.28), channel_id=1, source_target_pairs={{0,2},{1,3},{2,4},{3,5},{4,6},{5,7},{6,0},{7,1},{8,10},{9,11},{10,... | collective-permute-start | bytes 24584 | tf_op jit(solution)/shard_map/ppermute | solution.py:309
  48.7 5.2 %collective-permute-start.5 = (bf16[8,512]{1,0:T(8,128)(2,1)S(1)}, bf16[8,512]{1,0:T(8,128)(2,1)S(1)}, u32[]{:S(2)}, u32[]{:S(2)}) collective-permute-start(bf16[8,512]{1,0:T(8,128)(2,1)S(1)} %get-tuple-element.29), channel_id=1, source_target_pairs={{0,4},{1,5},{2,6},{3,7},{4,0},{5,1},{6,2},{7,3},{8,12},{9,13},{10,... | collective-permute-start | bytes 24584 | tf_op jit(solution)/shard_map/ppermute | solution.py:309
  51.5 3.7 %collective-permute-start.6 = (bf16[8,512]{1,0:T(8,128)(2,1)S(1)}, bf16[8,512]{1,0:T(8,128)(2,1)S(1)}, u32[]{:S(2)}, u32[]{:S(2)}) collective-permute-start(bf16[8,512]{1,0:T(8,128)(2,1)S(1)} %get-tuple-element.30), channel_id=1, source_target_pairs={{0,6},{1,7},{2,0},{3,1},{4,2},{5,3},{6,4},{7,5},{8,14},{9,15},{10,... | collective-permute-start | bytes 24584 | tf_op jit(solution)/shard_map/ppermute | solution.py:309

commit v7 on v6

--- a/solution.py
+++ b/solution.py
@@ -76,9 +76,11 @@
     for p in range(slots):
         source = place_ref[p, 0]
         at = pl.ds(pl.multiple_of((lax.rem(source, row_requests) // 2) * 16, 16), 16)
-        pair = row_refs[0][at, :]
-        for k in range(1, ring_y):
-            pair = jnp.where(source // row_requests == k, row_refs[k][at, :], pair)
+        back = source // row_requests
+        odd = lax.rem(back, 2) == 1
+        near = jnp.where(odd, row_refs[1][at, :], row_refs[0][at, :])
+        far = jnp.where(odd, row_refs[3][at, :], row_refs[2][at, :])
+        pair = jnp.where(back >= 2, far, near)
         both = lax.dot_general(
             pair, key_ref[p], (((1,), (1,)), ((), ())), preferred_element_type=f32
         )

time: 55.9 us -> 55.9 us (level)
  no operation moved by 1% of the time
where the time goes in v7:
time: 55.9 us; the launch traced here: 55.7 us
  blocking collectives  33.2 us (59%)
  starting transfers between devices  11 us (20%)
  waiting for transfers between devices  6.25 us (11%)
  Pallas kernels  3.9 us (7%)
  local copies, waits for them, and re-layouts  0.75 us (1%)
  other arithmetic  0.61 us (1%)
    all_to_all x1, blocking collectives, body(): lax.all_to_all(sent.reshape(n_inst, sent_rows, head_dim), inst, 0, 0, til...  17.2 us
    all_to_all x1, blocking collectives, body(): lax.all_to_all(copies, 'z', 0, 0, tiled=True)  15.9 us
    ppermute x3, starting transfers between devices, body(): total = total + lax.ppermute(parts[k - 1], 'tp', pairs).astype(f32)  5.73 us
    ppermute x3, starting transfers between devices, body(): from_rows[k] = lax.ppermute(row, 'y', pairs)  5.22 us
    ppermute x3, waiting for transfers between devices, body(): from_rows[k] = lax.ppermute(row, 'y', pairs)  3.48 us
    ppermute x3, waiting for transfers between devices, body(): total = total + lax.ppermute(parts[k - 1], 'tp', pairs).astype(f32)  2.22 us
    pallas_call x1, Pallas kernels, body(): pl.pallas_call(attend_kernel, out_shape=(shape((n_inst * sent_rows, head_...  1.18 us
  transfers between devices with their start and end apart: 7, of which 5 were waited for; matrix products, arithmetic and copies ran while one was open for 0% of the time, Pallas kernels for 3%

profile of v7, /device:TPU:32, one launch (start us, length us, event | category | flops | bytes accessed | tf_op | source)
XLA Modules:
  0.0 55.7 jit_solution(12026866470006193401)
XLA Ops:
  0.0 0.7 %copy-done.3 = bf16[8,8,128]{2,1,0:T(8,128)(2,1)S(1)} copy-done((bf16[8,8,128]{2,1,0:T(8,128)(2,1)S(1)}, bf16[8,8,128]{2,1,0:T(8,128)(2,1)}, u32[]{:S(2)}) %copy-start.3) | copy-done | bytes 16408
  0.7 15.9 %all_to_all.10 = bf16[8,64,128]{2,1,0:T(8,128)(2,1)S(1)} all-to-all(bf16[8,64,128]{2,1,0:T(8,128)(2,1)S(1)} %copies.1), channel_id=1, replica_groups=mesh['y'=4,'z'=8,'tp'=8] {'z'}, dimensions={0} | all-to-all | bytes 262144 | tf_op jit(solution)/shard_map/all_to_all | solution.py:236
  16.7 1.6 %collective-permute-start.2 = (bf16[512,128]{1,0:T(8,128)(2,1)S(1)}, bf16[512,128]{1,0:T(8,128)(2,1)S(1)}, u32[]{:S(2)}, u32[]{:S(2)}) collective-permute-start(bf16[512,128]{1,0:T(8,128)(2,1)S(1)} %bitcast.11), channel_id=1, source_target_pairs={{0,64},{64,128},{128,192},{192,0},{1,65},{65,129},{129,193},{193,1... | collective-permute-start | bytes 393224 | tf_op jit(solution)/shard_map/ppermute | solution.py:240
  18.3 1.7 %collective-permute-start.1 = (bf16[512,128]{1,0:T(8,128)(2,1)S(1)}, bf16[512,128]{1,0:T(8,128)(2,1)S(1)}, u32[]{:S(2)}, u32[]{:S(2)}) collective-permute-start(bf16[512,128]{1,0:T(8,128)(2,1)S(1)} %bitcast.12), channel_id=1, source_target_pairs={{0,192},{64,0},{128,64},{192,128},{1,193},{65,1},{129,65},{193,129... | collective-permute-start | bytes 393224 | tf_op jit(solution)/shard_map/ppermute | solution.py:240
  19.9 2.0 %collective-permute-start = (bf16[512,128]{1,0:T(8,128)(2,1)S(1)}, bf16[512,128]{1,0:T(8,128)(2,1)S(1)}, u32[]{:S(2)}, u32[]{:S(2)}) collective-permute-start(bf16[512,128]{1,0:T(8,128)(2,1)S(1)} %bitcast.13), channel_id=1, source_target_pairs={{0,128},{64,192},{128,0},{192,64},{1,129},{65,193},{129,1},{193,65... | collective-permute-start | bytes 393224 | tf_op jit(solution)/shard_map/ppermute | solution.py:240
  21.9 0.0 copy-done.7
  21.9 0.0 copy-done.8
  21.9 0.0 copy-done.9
  21.9 1.0 %plan.1 = (s32[32,128]{1,0:T(8,128)S(1)}, s32[32,128]{1,0:T(8,128)S(1)}, f32[32,128]{1,0:T(8,128)S(1)}, f32[32,128]{1,0:T(8,128)S(1)}) custom-call(s32[32]{0:T(128)S(1)} %copy-done.8, s32[32]{0:T(128)S(1)} %copy-done.9, s32[256]{0:T(256)S(1)} %copy-done.7, bf16[512,128]{1,0:T(8,128)(2,1)S(1)} %bitcast.14), custom_call_target="tpu_custom_call" | custom-call | flops 2000000000 | bytes 100000 | tf_op jit(solution)/shard_map/plan/pallas_call | solution.py:241
  22.9 1.1 %collective-permute-done.2.row1_ref = bf16[512,128]{1,0:T(8,128)(2,1)S(1)} collective-permute-done((bf16[512,128]{1,0:T(8,128)(2,1)S(1)}, bf16[512,128]{1,0:T(8,128)(2,1)S(1)}, u32[]{:S(2)}, u32[]{:S(2)}) %collective-permute-start.2) | collective-permute-done | bytes 131104 | tf_op jit(solution)/shard_map/ppermute | solution.py:240
  24.0 0.0 collective-permute-done.1.row3_ref
  24.0 2.4 %collective-permute-done.row2_ref = bf16[512,128]{1,0:T(8,128)(2,1)S(1)} collective-permute-done((bf16[512,128]{1,0:T(8,128)(2,1)S(1)}, bf16[512,128]{1,0:T(8,128)(2,1)S(1)}, u32[]{:S(2)}, u32[]{:S(2)}) %collective-permute-start) | collective-permute-done | bytes 131104 | tf_op jit(solution)/shard_map/ppermute | solution.py:240
  26.4 0.0 copy-done.1
  26.4 0.0 copy-done.2
  26.4 0.0 copy-start.6
  26.4 1.2 %attend.1 = (bf16[1280,128]{1,0:T(8,128)(2,1)S(1)}, f32[32,8,128]{2,1,0:T(8,128)S(1)}, f32[8,8,128]{2,1,0:T(8,128)S(1)}) custom-call(s32[32,128]{1,0:T(8,128)S(1)} %get-tuple-element.18.place_ref, s32[32,128]{1,0:T(8,128)S(1)} %get-tuple-element.19.limit_ref, f32[32,128]{1,0:T(8,128)S(1)} %get-tuple-element.20.sent_id_ref, ...), custom_call_target="tpu_custom_call" | custom-call | tf_op jit(solution)/shard_map/attend/pallas_call | solution.py:255
  27.6 17.2 %all_to_all.11 = bf16[32,40,128]{2,1,0:T(8,128)(2,1)S(1)} all-to-all(bf16[32,40,128]{2,1,0:T(8,128)(2,1)S(1)} %bitcast.16), channel_id=1, replica_groups=mesh['y'=4,'z'=8,'tp'=8] {'y','z'}, dimensions={0} | all-to-all | bytes 655360 | tf_op jit(solution)/shard_map/all_to_all | solution.py:271
  44.8 0.0 copy-done
  44.8 0.0 copy-done.4
  44.9 0.0 copy-done.5
  44.9 0.0 copy-done.6
  44.9 1.0 %merge.1 = (bf16[8,1024]{1,0:T(8,128)(2,1)S(1)}, bf16[8,2048]{1,0:T(8,128)(2,1)S(1)}) custom-call(bf16[1280,128]{1,0:T(8,128)(2,1)S(1)} %bitcast.10, f32[32,8,128]{2,1,0:T(8,128)S(1)} %get-tuple-element.23.local_out_ref, f32[8,8,128]{2,1,0:T(8,128)S(1)} %get-tuple-element.24.local_note_ref, bf16[64,128]{1,0:T(8,128)(2,1)S(1)} %bitcast.18, ...), custom_call_target="tpu_custom_call" | custom-call | tf_op jit(solution)/shard_map/merge/pallas_call | solution.py:274
  45.9 0.0 collective-permute-start.3
  45.9 0.7 %project.1.keep_ref = f32[8,2048]{1,0:T(8,128)S(1)} custom-call(bf16[8,1024]{1,0:T(8,128)(2,1)S(1)} %get-tuple-element.25.attended_ref, bf16[1024,4096]{1,0:T(8,128)(2,1)S(1)} %copy-done), custom_call_target="tpu_custom_call" | custom-call | flops 200000000 | bytes 4000000 | tf_op jit(solution)/shard_map/project/pallas_call | solution.py:290
  46.6 0.6 collective-permute-done.3.got_ref
  47.1 1.6 %collective-permute-start.4 = (bf16[8,512]{1,0:T(8,128)(2,1)S(1)}, bf16[8,512]{1,0:T(8,128)(2,1)S(1)}, u32[]{:S(2)}, u32[]{:S(2)}) collective-permute-start(bf16[8,512]{1,0:T(8,128)(2,1)S(1)} %get-tuple-element.28), channel_id=1, source_target_pairs={{0,2},{1,3},{2,4},{3,5},{4,6},{5,7},{6,0},{7,1},{8,10},{9,11},{10,... | collective-permute-start | bytes 24584 | tf_op jit(solution)/shard_map/ppermute | solution.py:311
  48.7 2.7 %collective-permute-start.5 = (bf16[8,512]{1,0:T(8,128)(2,1)S(1)}, bf16[8,512]{1,0:T(8,128)(2,1)S(1)}, u32[]{:S(2)}, u32[]{:S(2)}) collective-permute-start(bf16[8,512]{1,0:T(8,128)(2,1)S(1)} %get-tuple-element.29), channel_id=1, source_target_pairs={{0,4},{1,5},{2,6},{3,7},{4,0},{5,1},{6,2},{7,3},{8,12},{9,13},{10,... | collective-permute-start | bytes 24584 | tf_op jit(solution)/shard_map/ppermute | solution.py:311
  51.4 1.4 %collective-permute-start.6 = (bf16[8,512]{1,0:T(8,128)(2,1)S(1)}, bf16[8,512]{1,0:T(8,128)(2,1)S(1)}, u32[]{:S(2)}, u32[]{:S(2)}) collective-permute-start(bf16[8,512]{1,0:T(8,128)(2,1)S(1)} %get-tuple-element.30), channel_id=1, source_target_pairs={{0,6},{1,7},{2,0},{3,1},{4,2},{5,3},{6,4},{7,5},{8,14},{9,15},{10,... | collective-permute-start | bytes 24584 | tf_op jit(solution)/shard_map/ppermute | solution.py:311
  52.9 0.0 collective-permute-done.4
  52.9 1.0 %collective-permute-done.5 = bf16[8,512]{1,0:T(8,128)(2,1)S(1)} collective-permute-done((bf16[8,512]{1,0:T(8,128)(2,1)S(1)}, bf16[8,512]{1,0:T(8,128)(2,1)S(1)}, u32[]{:S(2)}, u32[]{:S(2)}) %collective-permute-start.5) | collective-permute-done | bytes 8224 | tf_op jit(solution)/shard_map/ppermute | solution.py:311
  53.9 1.2 %collective-permute-done.6 = bf16[8,512]{1,0:T(8,128)(2,1)S(1)} collective-permute-done((bf16[8,512]{1,0:T(8,128)(2,1)S(1)}, bf16[8,512]{1,0:T(8,128)(2,1)S(1)}, u32[]{:S(2)}, u32[]{:S(2)}) %collective-permute-start.6) | collective-permute-done | bytes 8224 | tf_op jit(solution)/shard_map/ppermute | solution.py:311
  55.1 0.6 %add_convert_fusion = bf16[8,512]{1,0:T(8,128)(2,1)} fusion(bf16[8,512]{1,0:T(8,128)(2,1)S(1)} %collective-permute-done.6, bf16[8,512]{1,0:T(8,128)(2,1)S(1)} %collective-permute-done.5, f32[8,512]{1,0:T(8,128)S(1)} %get-tuple-element.27, bf16[8,512]{1,0:T(8,128)(2,1)S(1)} %collective-permute-done.4), kind=kLoop, calls=%fused_computation | loop fusion | flops 28672 | bytes 49152 | tf_op jit(solution)/shard_map/convert_element_type | solution.py:312
  (11 shorter events, 0.0 us)
Async XLA Ops:
  0.0 0.7 %copy-start.3 = (bf16[8,8,128]{2,1,0:T(8,128)(2,1)S(1)}, bf16[8,8,128]{2,1,0:T(8,128)(2,1)}, u32[]{:S(2)}) copy-start(bf16[8,8,128]{2,1,0:T(8,128)(2,1)} %param.9) | copy-start | bytes 49156
  0.7 21.2 %copy-start.7 = (s32[256]{0:T(256)S(1)}, s32[256]{0:T(256)}, u32[]{:S(2)}) copy-start(s32[256]{0:T(256)} %length_ref.1) | copy-start | bytes 3076
  0.7 21.2 %copy-start.8 = (s32[32]{0:T(128)S(1)}, s32[32]{0:T(128)}, u32[]{:S(2)}) copy-start(s32[32]{0:T(128)} %owner_ref.1) | copy-start | bytes 388
  0.7 21.2 %copy-start.9 = (s32[32]{0:T(128)S(1)}, s32[32]{0:T(128)}, u32[]{:S(2)}) copy-start(s32[32]{0:T(128)} %index_ref.1) | copy-start | bytes 388
  16.7 9.7 %copy-start.1 = (bf16[32,256,1,128]{3,1,2,0:T(8,128)(2,1)S(1)}, bf16[32,256,1,128]{3,1,2,0:T(8,128)(2,1)}, u32[]{:S(2)}) copy-start(bf16[32,256,1,128]{3,1,2,0:T(8,128)(2,1)} %param.12) | copy-start | bytes 6291460
  16.7 9.7 %copy-start.2 = (bf16[32,256,1,128]{3,1,2,0:T(8,128)(2,1)S(1)}, bf16[32,256,1,128]{3,1,2,0:T(8,128)(2,1)}, u32[]{:S(2)}) copy-start(bf16[32,256,1,128]{3,1,2,0:T(8,128)(2,1)} %param.13) | copy-start | bytes 6291460
  16.7 7.3 %collective-permute-start.2 = (bf16[512,128]{1,0:T(8,128)(2,1)S(1)}, bf16[512,128]{1,0:T(8,128)(2,1)S(1)}, u32[]{:S(2)}, u32[]{:S(2)}) collective-permute-start(bf16[512,128]{1,0:T(8,128)(2,1)S(1)} %bitcast.11), channel_id=1, source_target_pairs={{0,64},{64,128},{128,192},{192,0},{1,65},{65,129},{129,193},{193,1... | collective-permute-start | bytes 393224 | tf_op jit(solution)/shard_map/ppermute | solution.py:240
  18.3 5.7 %collective-permute-start.1 = (bf16[512,128]{1,0:T(8,128)(2,1)S(1)}, bf16[512,128]{1,0:T(8,128)(2,1)S(1)}, u32[]{:S(2)}, u32[]{:S(2)}) collective-permute-start(bf16[512,128]{1,0:T(8,128)(2,1)S(1)} %bitcast.12), channel_id=1, source_target_pairs={{0,192},{64,0},{128,64},{192,128},{1,193},{65,1},{129,65},{193,129... | collective-permute-start | bytes 393224 | tf_op jit(solution)/shard_map/ppermute | solution.py:240
  19.9 6.5 %collective-permute-start = (bf16[512,128]{1,0:T(8,128)(2,1)S(1)}, bf16[512,128]{1,0:T(8,128)(2,1)S(1)}, u32[]{:S(2)}, u32[]{:S(2)}) collective-permute-start(bf16[512,128]{1,0:T(8,128)(2,1)S(1)} %bitcast.13), channel_id=1, source_target_pairs={{0,128},{64,192},{128,0},{192,64},{1,129},{65,193},{129,1},{193,65... | collective-permute-start | bytes 393224 | tf_op jit(solution)/shard_map/ppermute | solution.py:240
  21.9 22.9 %copy-start = (bf16[1024,4096]{1,0:T(8,128)(2,1)S(1)}, bf16[1024,4096]{1,0:T(8,128)(2,1)}, u32[]{:S(2)}) copy-start(bf16[1024,4096]{1,0:T(8,128)(2,1)} %weight_ref.3) | copy-start | bytes 25165828
  26.4 18.4 %copy-start.4 = (bf16[8,8,128]{2,1,0:T(8,128)(2,1)S(1)}, bf16[8,8,128]{2,1,0:T(8,128)(2,1)}, u32[]{:S(2)}) copy-start(bf16[8,8,128]{2,1,0:T(8,128)(2,1)} %param.9) | copy-start | bytes 49156
  26.4 18.4 %copy-start.5 = (bf16[8,1,128]{2,0,1:T(8,128)(2,1)S(1)}, bf16[8,1,128]{2,0,1:T(8,128)(2,1)}, u32[]{:S(2)}) copy-start(bf16[8,1,128]{2,0,1:T(8,128)(2,1)} %param.10) | copy-start | bytes 6148
  26.4 18.4 %copy-start.6 = (bf16[8,1,128]{2,0,1:T(8,128)(2,1)S(1)}, bf16[8,1,128]{2,0,1:T(8,128)(2,1)}, u32[]{:S(2)}) copy-start(bf16[8,1,128]{2,0,1:T(8,128)(2,1)} %param.11) | copy-start | bytes 6148
  45.9 1.2 %collective-permute-start.3 = (bf16[8,2048]{1,0:T(8,128)(2,1)S(1)}, bf16[8,2048]{1,0:T(8,128)(2,1)S(1)}, u32[]{:S(2)}, u32[]{:S(2)}) collective-permute-start(bf16[8,2048]{1,0:T(8,128)(2,1)S(1)} %get-tuple-element.26), channel_id=1, source_target_pairs={{0,1},{1,0},{2,3},{3,2},{4,5},{5,4},{6,7},{7,6},{8,9},{9,8},{10,11... | collective-permute-start | bytes 98312 | tf_op jit(solution)/shard_map/ppermute | solution.py:289
  47.1 5.7 %collective-permute-start.4 = (bf16[8,512]{1,0:T(8,128)(2,1)S(1)}, bf16[8,512]{1,0:T(8,128)(2,1)S(1)}, u32[]{:S(2)}, u32[]{:S(2)}) collective-permute-start(bf16[8,512]{1,0:T(8,128)(2,1)S(1)} %get-tuple-element.28), channel_id=1, source_target_pairs={{0,2},{1,3},{2,4},{3,5},{4,6},{5,7},{6,0},{7,1},{8,10},{9,11},{10,... | collective-permute-start | bytes 24584 | tf_op jit(solution)/shard_map/ppermute | solution.py:311
  48.7 5.2 %collective-permute-start.5 = (bf16[8,512]{1,0:T(8,128)(2,1)S(1)}, bf16[8,512]{1,0:T(8,128)(2,1)S(1)}, u32[]{:S(2)}, u32[]{:S(2)}) collective-permute-start(bf16[8,512]{1,0:T(8,128)(2,1)S(1)} %get-tuple-element.29), channel_id=1, source_target_pairs={{0,4},{1,5},{2,6},{3,7},{4,0},{5,1},{6,2},{7,3},{8,12},{9,13},{10,... | collective-permute-start | bytes 24584 | tf_op jit(solution)/shard_map/ppermute | solution.py:311
  51.4 3.7 %collective-permute-start.6 = (bf16[8,512]{1,0:T(8,128)(2,1)S(1)}, bf16[8,512]{1,0:T(8,128)(2,1)S(1)}, u32[]{:S(2)}, u32[]{:S(2)}) collective-permute-start(bf16[8,512]{1,0:T(8,128)(2,1)S(1)} %get-tuple-element.30), channel_id=1, source_target_pairs={{0,6},{1,7},{2,0},{3,1},{4,2},{5,3},{6,4},{7,5},{8,14},{9,15},{10,... | collective-permute-start | bytes 24584 | tf_op jit(solution)/shard_map/ppermute | solution.py:311
